TPU v7x, 32 devices: a whole 2x2x4 slice. The times are simulated.
32 devices in a mesh: prompt: 1, seq: 32 (over z, y, x, core).
Axes of the slice: x: 2, y: 2, z: 4, core: 2. Of those that a mesh axis runs over, the one named last changes fastest.
Arguments:
- queries: bfloat16 [8192, 32, 128], P(('prompt', 'seq')), may hold values from -12 to 12
- key_value: bfloat16 [2, 8192, 16, 128], P(None, ('prompt', 'seq')), may hold values from -6 to 6
- damping: bfloat16 [8192], P('prompt'), may hold values from 0.0099487305 to 1
- span_start: int32 [1], P('prompt'), may hold values from 0 to 3584
- steered_heads: int32 [8], replicated, may hold values from 0 to 31, as said below
Outputs:
- attention: bfloat16 [8192, 32, 128], P(('prompt', 'seq'))
Inputs may be any that keep to these rules, and one draw needn't show every extreme that they name: The emphasized tokens are span_start to span_start + 511. `steered_heads`: 8 distinct head numbers in any order; head 31 is always one of them.
All inputs are finite; a program needn't handle non-finite values.
Results may differ from a plain program's by a relative error of at most 0.0085.
Values may be sent and summed in bfloat16 or wider, within the bound.
No kernel may reach another device: no remote copies, remote signals or barrier semaphores. Data moves between devices by JAX's collectives and lax.ppermute only.
A program may use at most 64 MiB of HBM per device.

v0:
```python
import functools
import math

import jax
import jax.numpy as jnp
from jax import lax
from jax.experimental import pallas as pl
from jax.experimental.pallas import tpu as pltpu
from jax.sharding import PartitionSpec as P

WINDOW = 4096
SPAN = 512

SCORE_SCALE = 144.0 ** (-0.5)
SOFTCAP = 50.0
LOG2_E = math.log2(math.e)

GROUP = 8
CHUNK = 64
TOKEN_STEPS = 4
PAIR_FLOPS = 256
VMEM_BYTES = 48 * 1024 * 1024

FIRST_SCALAR = 32
PLANE, SPAN_FIRST, STEERED_0, STEERED_1 = range(FIRST_SCALAR, FIRST_SCALAR + 4)
SCALARS = FIRST_SCALAR + 4


def smem():
    return pl.BlockSpec(memory_space=pltpu.SMEM)


def vmem():
    return pl.BlockSpec(memory_space=pltpu.VMEM)


def in_hbm(operand):
    return pltpu.with_memory_space_constraint(operand, pltpu.HBM)


def params():
    return pltpu.CompilerParams(vmem_limit_bytes=VMEM_BYTES)


def cost(pairs, moved):
    return pl.CostEstimate(
        flops=int(pairs * PAIR_FLOPS), bytes_accessed=int(moved), transcendentals=int(2 * pairs)
    )


def pack_kernel(
    index_ref, span_ref, steered_ref, queries_ref, states_ref,
    both_a, states_b, all_b, scalars, query_heads, state_heads,
):
    key_heads = states_ref.shape[2]
    steered_count = steered_ref.shape[0]

    @pl.when(pl.program_id(0) == 0)
    def _():
        steered_keys = [lax.div(steered_ref[n], 2) for n in range(steered_count)]
        flags = []
        for head in range(key_heads):
            hit = steered_keys[0] == head
            for n in range(1, steered_count):
                hit = hit | (steered_keys[n] == head)
            flags.append(hit.astype(jnp.int32))
        total = sum(flags[1:], flags[0])
        before = jnp.int32(0)
        for head in range(key_heads):
            rank = jnp.where(flags[head] == 1, before, total + head - before)
            scalars[rank] = jnp.int32(head)
            before = before + flags[head]
        place = lax.rem(index_ref[0], GROUP)
        scalars[PLANE] = lax.div(index_ref[0], GROUP)
        scalars[SPAN_FIRST] = span_ref[0]
        own_head = scalars[place]
        for group_head in range(2):
            hit = steered_ref[0] == 2 * own_head + group_head
            for n in range(1, steered_count):
                hit = hit | (steered_ref[n] == 2 * own_head + group_head)
            scalars[STEERED_0 + group_head] = hit.astype(jnp.int32)

    for part in range(2):
        state_heads[part] = jnp.transpose(states_ref[part], (1, 0, 2))
        for n in range(GROUP):
            both_a[n, part] = state_heads[part, scalars[n]]
            state = state_heads[part, scalars[GROUP + n]]
            states_b[n, part] = state
            all_b[n, 2 + part] = state
    query_heads[...] = jnp.transpose(queries_ref[...], (1, 0, 2))
    for n in range(GROUP):
        for group_head in range(2):
            both_a[n, 2 + group_head] = query_heads[2 * scalars[n] + group_head]
            all_b[n, 4 + group_head] = query_heads[2 * scalars[GROUP + n] + group_head]


def pack(index, span_start, steered_heads, queries, states):
    rows, heads, width = queries.shape
    key_heads = states.shape[2]
    some = rows // TOKEN_STEPS


    def sent(parts):
        shape = pltpu.HBM((GROUP, parts, rows, width), queries.dtype)
        return shape, pl.BlockSpec((GROUP, parts, some, width), lambda n: (0, 0, n, 0))

    shapes, specs = zip(sent(4), sent(2), sent(6))
    return pl.pallas_call(
        pack_kernel,
        grid=(TOKEN_STEPS,),
        in_specs=[smem()] * 3
        + [
            pl.BlockSpec((some, heads, width), lambda n: (n, 0, 0)),
            pl.BlockSpec((2, some, key_heads, width), lambda n: (0, n, 0, 0)),
        ],
        out_specs=list(specs) + [smem()],
        out_shape=list(shapes) + [jax.ShapeDtypeStruct((SCALARS,), jnp.int32)],
        scratch_shapes=[
            pltpu.VMEM((heads, some, width), queries.dtype),
            pltpu.VMEM((2, key_heads, some, width), queries.dtype),
        ],
        compiler_params=params(),
        cost_estimate=cost(0, 4 * (queries.size + states.size)),
    )(index, span_start, steered_heads, in_hbm(queries), in_hbm(states))


def raw_scores(query, key):
    return lax.dot_general(
        query, key, (((1,), (1,)), ((), ())), preferred_element_type=jnp.float32
    )


def weights(raw_score, bias, visible):
    score = jnp.tanh(raw_score * (SCORE_SCALE / SOFTCAP)) * (SOFTCAP * LOG2_E)
    weight = jnp.exp2(score if bias is None else score + bias)
    return weight if visible is None else jnp.where(visible, weight, 0.0)


def lane_sums(weight, lanes):
    sums = weight[:, :lanes]
    for first in range(lanes, weight.shape[1], lanes):
        sums = sums + weight[:, first : first + lanes]
    return sums


def attend_kernel(*refs, step, steerable, last):
    refs = list(refs)
    scalars = refs.pop(0)
    bias_ref = refs.pop(0) if steerable else None
    low_ref, high_ref, states_ref = refs.pop(0), refs.pop(0), refs.pop(0)
    span_ref = refs.pop(0) if steerable and last else None
    if step:
        old_weighted, old_sums = refs.pop(0), refs.pop(0)
    if last:
        out_ref = refs.pop(0)
    weighted_ref, sums_ref, query_ref = refs[:3]
    around_ref, gathered_ref = refs[3:] if steerable and last else (None, None)
    low = pl.program_id(0)
    blocks, _, rows, width = states_ref.shape
    high = blocks - 1 - low
    plane = scalars[PLANE]
    first_block = (plane - step) * blocks
    query_ref[0] = low_ref[0].reshape(2 * rows, width)
    query_ref[1] = high_ref[0].reshape(2 * rows, width)
    if step:
        weighted_ref[...] = old_weighted[...]
        sums_ref[...] = old_sums[...]
    else:
        weighted_ref[...] = jnp.zeros(weighted_ref.shape, jnp.float32)
        sums_ref[...] = jnp.zeros(sums_ref.shape, jnp.float32)
    flags = [scalars[STEERED_0 + n] for n in range(2)]
    flag_values = [flag.astype(jnp.float32) for flag in flags]

    def states(part, key_block, count):
        if count == 1:
            return states_ref[key_block, part]
        return states_ref[pl.ds(key_block, count), part].reshape(count * rows, width)

    def bias(key_block, count):
        if not steerable:
            return None
        parts = [bias_ref[pl.ds(first_block + key_block + n, 1), :] for n in range(count)]
        row = parts[0] if count == 1 else jnp.concatenate(parts, axis=1)
        return [row * value for value in flag_values]

    def add(tiles):
        def of_span(key_block):
            return isinstance(key_block, int) and key_block < 0

        def part_of(part, key_block, count):
            if of_span(key_block):
                return gathered_ref[part, ~key_block]
            return states(part, key_block, count)

        def score(tile):
            which, key_block, count, _ = tile
            return raw_scores(query_ref[which], part_of(0, key_block, count))

        ahead = score(tiles[0])
        for n, (which, key_block, count, visible) in enumerate(tiles):
            raw_score = ahead
            if n + 1 < len(tiles):
                ahead = score(tiles[n + 1])
            added = None if of_span(key_block) else bias(key_block, count)
            chunk = CHUNK // count
            rounded = []
            for first in range(0, 2 * rows, chunk):
                head, row = first // rows, first % rows
                columns = slice(0, count * rows)
                if visible is in_order:
                    columns = slice(0, -(-(row + chunk) // width) * width)
                    if step:
                        columns = slice(row // width * width, rows)
                weight = weights(
                    raw_score[first : first + chunk, columns],
                    None if added is None else added[head][:, columns],
                    None if visible is None else visible(head, row, chunk)[:, columns],
                )
                some = pl.ds(first, chunk)
                sums_ref[0, which, some, :] += lane_sums(weight, width)
                weight = weight.astype(jnp.bfloat16)
                sides = [
                    jnp.zeros((chunk, size), jnp.bfloat16)
                    for size in (columns.start, count * rows - columns.stop)
                ]
                parts = [part for part in (sides[0], weight, sides[1]) if part.shape[1]]
                rounded.append(parts[0] if len(parts) == 1 else jnp.concatenate(parts, axis=1))
            weighted_ref[0, which] += jnp.dot(
                jnp.concatenate(rounded, axis=0),
                part_of(1, key_block, count),
                preferred_element_type=jnp.float32,
            )

    def gather_span():
        start = scalars[SPAN_FIRST] - first_block * rows
        pad = SPAN // rows
        for part in range(2):
            before = span_ref[part].astype(jnp.float32)

            @pl.when(start < 0)
            def _():
                around_ref[:SPAN, :] = before
                for n in range(2):
                    around_ref[SPAN + n * rows : SPAN + (n + 1) * rows, :] = states_ref[
                        n, part
                    ].astype(jnp.float32)

            block = jnp.clip(lax.div(jnp.maximum(start, 0), rows), 0, blocks - pad - 1)

            @pl.when(start >= 0)
            def _():
                for n in range(pad + 1):
                    around_ref[n * rows : (n + 1) * rows, :] = states_ref[
                        block + n, part
                    ].astype(jnp.float32)
                around_ref[(pad + 1) * rows :, :] = jnp.zeros((SPAN, width), jnp.float32)

            offset = jnp.where(start < 0, jnp.maximum(start + SPAN, 0), start - block * rows)
            for n in range(pad):
                gathered_ref[part, n] = around_ref[pl.ds(offset + n * rows, rows), :].astype(
                    jnp.bfloat16
                )

    def ranks(row, count):
        shape = (count, rows)
        return (
            row
            + lax.broadcasted_iota(jnp.int32, shape, 0)
            - lax.broadcasted_iota(jnp.int32, shape, 1)
        )

    def in_order(head, row, count):
        return ranks(row, count) >= 0 if step == 0 else ranks(row, count) < 0

    def span_tiles():
        tiles = []
        for which, block in ((0, low), (1, high)):
            for n in range(SPAN // rows):
                nearest = scalars[SPAN_FIRST] + n * rows + WINDOW - (plane * blocks + block) * rows
                least = [jnp.where(flag == 1, nearest, 2 * rows) for flag in flags]

                def visible(head, row, count, least=least):
                    return ranks(row, count) >= least[head]

                tiles.append((which, ~n, 1, visible))
        return tiles

    def compute():
        if step == 1:
            add([(which, n, 2, None) for which in range(2) for n in range(0, blocks, 2)])
            return
        tiles = []
        for n in range(blocks - 1):
            if step == 0:
                is_low = n < low
                tiles.append((jnp.where(is_low, 0, 1), jnp.where(is_low, n, n - low), 1, None))
            else:
                is_high = n < low
                tiles.append(
                    (jnp.where(is_high, 1, 0), jnp.where(is_high, high + 1 + n, n + 1), 1, None)
                )

        for which, block in ((0, low), (1, high)):
            tiles.append((which, block, 1, in_order))
        if not (steerable and last):
            add(tiles)
            return
        wanted = flags[0] + flags[1] > 0
        wanted = wanted & (scalars[SPAN_FIRST] < (first_block + blocks) * rows)
        pl.when(wanted & (low == 0))(gather_span)
        pl.when(wanted)(lambda: add(tiles + span_tiles()))
        pl.when(jnp.logical_not(wanted))(lambda: add(tiles))

    if step:
        pl.when(plane >= step)(compute)
    else:
        compute()
    if last:
        write_result(out_ref, weighted_ref, sums_ref, low, high)


def write_result(out_ref, weighted_ref, sums_ref, low, high):
    for which, block in ((0, low), (1, high)):
        total = jnp.sum(sums_ref[0, which], axis=-1, keepdims=True)
        result = (weighted_ref[0, which] / total).astype(out_ref.dtype)
        out_ref[block] = result.reshape(out_ref.shape[1:])


def query_specs(queries):
    blocks, parts, rows, width = queries.shape
    one, at = (1, 2, rows, width), parts // 2 - 1
    return [
        pl.BlockSpec(one, lambda n: (n, at, 0, 0)),
        pl.BlockSpec(one, lambda n: (blocks - 1 - n, at, 0, 0)),
    ]


def held_spec(queries):
    _, _, rows, width = queries.shape
    return pl.BlockSpec((1, 2, 2 * rows, width), lambda n: (n, 0, 0, 0))


def attend(
    step, scalars, bias, queries, states, carried=None, span_states=None, last=False, states_at=0
):
    blocks, _, rows, width = queries.shape
    pair = 2
    assert blocks % 2 == 0
    held = pltpu.HBM((blocks // 2, 2, pair * rows, width), jnp.float32)
    whole = pl.BlockSpec((blocks, 2, rows, width), lambda n: (0, states_at, 0, 0))
    operands, in_specs = [scalars], [smem()]
    if bias is not None:
        operands.append(bias)
        in_specs.append(pl.BlockSpec(bias.shape, lambda n: (0, 0)))
    operands += [queries, queries, states]
    in_specs += query_specs(queries) + [whole]
    if span_states is not None:
        operands.append(span_states)
        in_specs.append(pl.BlockSpec(span_states.shape, lambda n: (0, 0, 0)))
    if carried is not None:
        operands += [in_hbm(sums) for sums in carried]
        in_specs += [held_spec(queries)] * 2
    scratch = [pltpu.VMEM((2, pair * rows, width), queries.dtype)]
    if span_states is not None:
        scratch.append(pltpu.VMEM((2 * SPAN + rows, width), jnp.float32))
        scratch.append(pltpu.VMEM((2, SPAN // rows, rows, width), queries.dtype))
    if last:
        out_shape = jax.ShapeDtypeStruct((blocks, pair, rows, width), queries.dtype)
        out_specs = pl.BlockSpec(out_shape.shape, lambda n: (0, 0, 0, 0))
        scratch = [pltpu.VMEM((1, 2, pair * rows, width), jnp.float32)] * 2 + scratch
    else:
        out_shape, out_specs = [held, held], [held_spec(queries)] * 2
    return pl.pallas_call(
        functools.partial(attend_kernel, step=step, steerable=bias is not None, last=last),
        grid=(blocks // 2,),
        in_specs=in_specs,
        out_specs=out_specs,
        out_shape=out_shape,
        scratch_shapes=scratch,
        compiler_params=params(),
        cost_estimate=cost(
            pair * (blocks * rows) ** 2 / (1 if step == 1 else 2),
            8 * queries.size + 8 * pair * blocks * rows * width,
        ),
    )(*operands)


def unpack_kernel(scalars, out_a, out_b, attention, heads_ref):
    for n in range(GROUP):
        for group_head in range(2):
            heads_ref[2 * scalars[n] + group_head] = out_a[n, group_head]
            heads_ref[2 * scalars[GROUP + n] + group_head] = out_b[n, group_head]
    attention[...] = jnp.transpose(heads_ref[...], (1, 0, 2))


def unpack(scalars, out_a, out_b):
    blocks, pair, rows, width = out_a.shape
    heads = 2 * blocks * pair
    return pl.pallas_call(
        unpack_kernel,
        in_specs=[smem(), vmem(), vmem()],
        out_specs=vmem(),
        out_shape=jax.ShapeDtypeStruct((rows, heads, width), out_a.dtype),
        scratch_shapes=[pltpu.VMEM((heads, rows, width), out_a.dtype)],
        compiler_params=params(),
        cost_estimate=cost(0, 8 * out_a.size),
    )(scalars, out_a, out_b)


def per_device(queries, key_value, damping, span_start, steered_heads):
    rows = queries.shape[0]
    device_count = lax.axis_size("seq")
    assert WINDOW == 2 * GROUP * rows and device_count == 4 * GROUP
    assert key_value.shape[2] == 2 * GROUP and queries.shape[1] == 4 * GROUP
    assert steered_heads.shape[0] <= GROUP
    groups = [
        list(range(first, first + GROUP)) for first in range(0, device_count, GROUP)
    ]

    def exchange(blocks):
        return lax.all_to_all(
            blocks, "seq", split_axis=0, concat_axis=0, axis_index_groups=groups, tiled=True
        )

    def onward(blocks, planes=1):
        shift = planes * GROUP
        pairs = [(n, n + shift) for n in range(device_count - shift)]
        return lax.ppermute(blocks, "seq", pairs)

    def after(value, earlier):
        return lax.optimization_barrier((value, earlier))[0]

    index = lax.axis_index("seq").astype(jnp.int32).reshape(1)
    both_a, states_b, all_b, scalars = pack(
        index, span_start, steered_heads, queries, key_value
    )
    position = jnp.arange(damping.shape[0], dtype=jnp.int32)
    emphasized = (position >= span_start[0]) & (position < span_start[0] + SPAN)
    bias = jnp.where(emphasized, 0.0, jnp.log2(damping.astype(jnp.float32)))
    bias = bias.reshape(-1, rows)

    raw_b = onward(states_b)
    both_a = exchange(both_a)
    states_a = both_a[:, :2]
    back_a = onward(after(states_a, raw_b))
    all_b = lax.dynamic_update_slice(all_b, after(raw_b, states_a), (0, 0, 0, 0))
    all_b = exchange(all_b)
    held_a = attend(0, scalars, bias, after(both_a, raw_b), both_a)
    far_a = onward(after(back_a, held_a))
    length = GROUP * rows
    span_states = lax.dynamic_slice_in_dim(
        after(both_a, (back_a, held_a))[:, :2].transpose(1, 0, 2, 3).reshape(2, length, -1),
        jnp.minimum(span_start[0], length - SPAN),
        SPAN,
        1,
    )
    span_states = onward(span_states, 3)
    held_a = attend(1, scalars, bias, both_a, back_a, held_a)
    all_b = after(all_b, held_a)
    far_b = onward(all_b[:, :2])
    held_b = attend(0, scalars, None, all_b, all_b, states_at=1)
    out_a = attend(
        2, scalars, bias, both_a, far_a, after(held_a, held_b), span_states, last=True
    )
    held_b = attend(1, scalars, None, all_b, all_b, after(held_b, out_a))
    out_a = exchange(out_a)
    out_b = attend(2, scalars, None, all_b, far_b, held_b, last=True)
    out_b = exchange(out_b)
    return unpack(scalars, out_a, out_b)


def solution(mesh):
    in_specs = (
        P(("prompt", "seq"), None, None),
        P(None, ("prompt", "seq"), None, None),
        P("prompt"),
        P("prompt"),
        P(),
    )
    out_specs = P(("prompt", "seq"), None, None)
    return jax.shard_map(
        per_device, mesh=mesh, in_specs=in_specs, out_specs=out_specs, check_vma=False
    )
```

profile of v0, /device:TPU:24, one launch (start us, length us, event | category | flops | bytes accessed | tf_op | source)
XLA Modules:
  0.0 168.2 jit_solution(5168881295510587611)
XLA Ops:
  0.7 0.0 copy-start
  0.7 0.6 copy-done
  1.3 6.5 %shard_map.55 = (bf16[8,4,256,128]{3,2,1,0:T(8,128)(2,1)}, bf16[8,2,256,128]{3,2,1,0:T(8,128)(2,1)}, bf16[8,6,256,128]{3,2,1,0:T(8,128)(2,1)}, s32[36]{0:T(128)S(1)}) custom-call(s32[1]{0:T(128)} %bitcast.index_ref, s32[1]{0:T(128)} %copy.8.span_ref, s32[8]{0:T(128)S(1)} %copy-done, bf16[256,32,128]{2,1,0:T(8,128)(2,1)} %queries_ref.1, ...), custom_call_target="tpu_custom_call" | custom-call | bytes 8388608 | tf_op jit(solution)/shard_map/pallas_call | solution.py:108
  7.8 3.7 %all-to-all-start = ((bf16[8,4,256,128]{3,2,1,0:T(8,128)(2,1)}), bf16[8,4,256,128]{3,2,1,0:T(8,128)(2,1)S(1)}, u32[]{:S(2)}, u32[]{:S(2)}) async-start(bf16[8,4,256,128]{3,2,1,0:T(8,128)(2,1)} %get-tuple-element.28), calls=%async_computation | async-start | bytes 4194304 | tf_op jit(solution)/shard_map/all_to_all | solution.py:421
  11.5 1.3 collective-permute-start
  12.8 25.4 %all-to-all-done.refs_2_.refs_3_.refs_4_ = bf16[8,4,256,128]{3,2,1,0:T(8,128)(2,1)S(1)} async-done(((bf16[8,4,256,128]{3,2,1,0:T(8,128)(2,1)}), bf16[8,4,256,128]{3,2,1,0:T(8,128)(2,1)S(1)}, u32[]{:S(2)}, u32[]{:S(2)}) %all-to-all-start) | async-done | bytes 2097184 | tf_op jit(solution)/shard_map/all_to_all | solution.py:421
  38.2 1.1 slice.12
  39.3 0.0 collective-permute-done
  39.3 1.2 constant_dynamic-update-slice_fusion
  40.4 0.0 copy-start.1
  40.4 4.6 %all-to-all-start.1 = ((bf16[8,6,256,128]{3,2,1,0:T(8,128)(2,1)}), bf16[8,6,256,128]{3,2,1,0:T(8,128)(2,1)}, u32[]{:S(2)}, u32[]{:S(2)}) async-start(bf16[8,6,256,128]{3,2,1,0:T(8,128)(2,1)} %constant_dynamic-update-slice_fusion), calls=%async_computation.1 | async-start | bytes 6291456 | tf_op jit(solution)/shard_map/all_to_all | solution.py:421
  45.0 1.3 collective-permute-start.1
  46.3 0.0 copy-done.1
  46.4 8.8 %shard_map.56 = (f32[4,2,512,128]{3,2,1,0:T(8,128)}, f32[4,2,512,128]{3,2,1,0:T(8,128)}) custom-call(s32[36]{0:T(128)S(1)} %get-tuple-element.27.refs_0_.scalars, f32[32,256]{1,0:T(8,128)S(1)} %reshape.10.refs_1_, bf16[8,4,256,128]{3,2,1,0:T(8,128)(2,1)S(1)} %all-to-all-done.refs_2_.refs_3_.refs_4_, ...), custom_call_target="tpu_custom_call" | custom-call | flops 1073741824 | bytes 12582912 | tf_op jit(solution)/shard_map/pallas_call | solution.py:373
  55.2 17.4 %collective-permute-done.1.refs_4_ = bf16[8,2,256,128]{3,2,1,0:T(8,128)(2,1)S(1)} collective-permute-done((bf16[8,2,256,128]{3,2,1,0:T(8,128)(2,1)}, bf16[8,2,256,128]{3,2,1,0:T(8,128)(2,1)S(1)}, u32[]{:S(2)}, u32[]{:S(2)}) %collective-permute-start.1) | collective-permute-done | bytes 1048608 | tf_op jit(solution)/shard_map/ppermute | solution.py:428
  72.6 1.3 collective-permute-start.2
  73.9 0.1 slice_bitcast_fusion
  73.9 0.1 copy.6
  74.0 0.8 constant_dynamic-slice_fusion
  74.8 1.3 collective-permute-start.3
  76.1 12.6 %shard_map.57 = (f32[4,2,512,128]{3,2,1,0:T(8,128)}, f32[4,2,512,128]{3,2,1,0:T(8,128)}) custom-call(s32[36]{0:T(128)S(1)} %get-tuple-element.27.refs_0_.scalars, f32[32,256]{1,0:T(8,128)S(1)} %reshape.10.refs_1_, bf16[8,4,256,128]{3,2,1,0:T(8,128)(2,1)S(1)} %all-to-all-done.refs_2_.refs_3_.refs_4_, ...), custom_call_target="tpu_custom_call" | custom-call | flops 2147483648 | bytes 12582912 | tf_op jit(solution)/shard_map/pallas_call | solution.py:373
  88.7 0.0 all-to-all-done.1.refs_1_.refs_2_.refs_3_
  88.7 2.3 %slice.11 = bf16[8,2,256,128]{3,2,1,0:T(8,128)(2,1)} slice(bf16[8,6,256,128]{3,2,1,0:T(8,128)(2,1)} %all-to-all-done.1.refs_1_.refs_2_.refs_3_), slice={[0:8], [0:2], [0:256], [0:128]} | slice | bytes 2097152 | tf_op jit(solution)/shard_map/slice | solution.py:460
  91.1 1.5 collective-permute-start.4
  92.5 9.5 %shard_map.58 = (f32[4,2,512,128]{3,2,1,0:T(8,128)}, f32[4,2,512,128]{3,2,1,0:T(8,128)}) custom-call(s32[36]{0:T(128)S(1)} %get-tuple-element.27.refs_0_.scalars, bf16[8,6,256,128]{3,2,1,0:T(8,128)(2,1)} %all-to-all-done.1.refs_1_.refs_2_.refs_3_, bf16[8,6,256,128]{3,2,1,0:T(8,128)(2,1)} %all-to-all-done.1.refs_1_.refs_2_.refs_3_, ...), custom_call_target="tpu_custom_call" | custom-call | flops 1073741824 | bytes 16777216 | tf_op jit(solution)/shard_map/pallas_call | solution.py:373
  102.1 3.9 %collective-permute-done.3.refs_5_ = bf16[2,512,128]{2,1,0:T(8,128)(2,1)S(1)} collective-permute-done((bf16[2,512,128]{2,1,0:T(8,128)(2,1)}, bf16[2,512,128]{2,1,0:T(8,128)(2,1)S(1)}, u32[]{:S(2)}, u32[]{:S(2)}) %collective-permute-start.3) | collective-permute-done | bytes 262176 | tf_op jit(solution)/shard_map/ppermute | solution.py:428
  106.0 0.3 collective-permute-done.2.refs_4_
  106.3 12.5 %shard_map.59 = bf16[8,2,256,128]{3,2,1,0:T(8,128)(2,1)} custom-call(s32[36]{0:T(128)S(1)} %get-tuple-element.27.refs_0_.scalars, f32[32,256]{1,0:T(8,128)S(1)} %reshape.10.refs_1_, bf16[8,4,256,128]{3,2,1,0:T(8,128)(2,1)S(1)} %all-to-all-done.refs_2_.refs_3_.refs_4_, bf16[8,4,256,128]{3,2,1,0:T(8,128)(2,1)S(1)} %all-to-all-done.refs_2_.refs_3_.refs_4_, ...), custom_call_target="tpu_custom_call" | custom-call | flops 1073741824 | bytes 12582912 | tf_op jit(solution)/shard_map/pallas_call | solution.py:373
  118.7 3.9 %all-to-all-start.2 = ((bf16[8,2,256,128]{3,2,1,0:T(8,128)(2,1)}), bf16[8,2,256,128]{3,2,1,0:T(8,128)(2,1)S(1)}, u32[]{:S(2)}, u32[]{:S(2)}) async-start(bf16[8,2,256,128]{3,2,1,0:T(8,128)(2,1)} %shard_map.59), calls=%async_computation.2 | async-start | bytes 2097152 | tf_op jit(solution)/shard_map/all_to_all | solution.py:421
  122.6 13.1 %shard_map.60 = (f32[4,2,512,128]{3,2,1,0:T(8,128)}, f32[4,2,512,128]{3,2,1,0:T(8,128)}) custom-call(s32[36]{0:T(128)S(1)} %get-tuple-element.27.refs_0_.scalars, bf16[8,6,256,128]{3,2,1,0:T(8,128)(2,1)} %all-to-all-done.1.refs_1_.refs_2_.refs_3_, bf16[8,6,256,128]{3,2,1,0:T(8,128)(2,1)} %all-to-all-done.1.refs_1_.refs_2_.refs_3_, ...), custom_call_target="tpu_custom_call" | custom-call | flops 2147483648 | bytes 16777216 | tf_op jit(solution)/shard_map/pallas_call | solution.py:373
  135.7 0.0 collective-permute-done.4.refs_3_
  135.7 10.2 %shard_map.61 = bf16[8,2,256,128]{3,2,1,0:T(8,128)(2,1)S(1)} custom-call(s32[36]{0:T(128)S(1)} %get-tuple-element.27.refs_0_.scalars, bf16[8,6,256,128]{3,2,1,0:T(8,128)(2,1)} %all-to-all-done.1.refs_1_.refs_2_.refs_3_, bf16[8,6,256,128]{3,2,1,0:T(8,128)(2,1)} %all-to-all-done.1.refs_1_.refs_2_.refs_3_, ...), custom_call_target="tpu_custom_call" | custom-call | flops 1073741824 | bytes 16777216 | tf_op jit(solution)/shard_map/pallas_call | solution.py:373
  146.0 0.0 all-to-all-done.2.out_a
  146.0 19.4 %all_to_all.20.out_b = bf16[8,2,256,128]{3,2,1,0:T(8,128)(2,1)S(1)} all-to-all(bf16[8,2,256,128]{3,2,1,0:T(8,128)(2,1)S(1)} %shard_map.61), channel_id=1, replica_groups={{0,1,2,3,4,5,6,7},{8,9,10,11,12,13,14,15},{16,17,18,19,20,21,22,23},{24..., dimensions={0} | all-to-all | bytes 2097152 | tf_op jit(solution)/shard_map/all_to_all | solution.py:421
  165.4 2.8 %shard_map.62 = bf16[256,32,128]{2,1,0:T(8,128)(2,1)} custom-call(s32[36]{0:T(128)S(1)} %get-tuple-element.27.refs_0_.scalars, bf16[8,2,256,128]{3,2,1,0:T(8,128)(2,1)S(1)} %all-to-all-done.2.out_a, bf16[8,2,256,128]{3,2,1,0:T(8,128)(2,1)S(1)} %all_to_all.20.out_b), custom_call_target="tpu_custom_call" | custom-call | bytes 4194304 | tf_op jit(solution)/shard_map/pallas_call | solution.py:399
  (2 shorter events, 0.0 us)
Async XLA Ops:
  0.7 0.7 copy-start
  7.8 30.4 %all-to-all-start = ((bf16[8,4,256,128]{3,2,1,0:T(8,128)(2,1)}), bf16[8,4,256,128]{3,2,1,0:T(8,128)(2,1)S(1)}, u32[]{:S(2)}, u32[]{:S(2)}) async-start(bf16[8,4,256,128]{3,2,1,0:T(8,128)(2,1)} %get-tuple-element.28), calls=%async_computation | async-start | bytes 4194304 | tf_op jit(solution)/shard_map/all_to_all | solution.py:421
  11.5 27.7 %collective-permute-start = (bf16[8,2,256,128]{3,2,1,0:T(8,128)(2,1)}, bf16[8,2,256,128]{3,2,1,0:T(8,128)(2,1)S(1)}, u32[]{:S(2)}, u32[]{:S(2)}) collective-permute-start(bf16[8,2,256,128]{3,2,1,0:T(8,128)(2,1)} %get-tuple-element.29), channel_id=1, source_target_pairs={{0,8},{1,9},{2,10},{3,11},{4,12},{5,13},{6,14},{7,15},{8,16},{9,17... | collective-permute-start | bytes 3145736 | tf_op jit(solution)/shard_map/ppermute | solution.py:428
  40.4 5.9 %copy-start.1 = (bf16[8192]{0:T(1024)(128)(2,1)S(1)}, bf16[8192]{0:T(1024)(128)(2,1)}, u32[]{:S(2)}) copy-start(bf16[8192]{0:T(1024)(128)(2,1)} %param.7) | copy-start | bytes 49156
  40.4 48.3 %all-to-all-start.1 = ((bf16[8,6,256,128]{3,2,1,0:T(8,128)(2,1)}), bf16[8,6,256,128]{3,2,1,0:T(8,128)(2,1)}, u32[]{:S(2)}, u32[]{:S(2)}) async-start(bf16[8,6,256,128]{3,2,1,0:T(8,128)(2,1)} %constant_dynamic-update-slice_fusion), calls=%async_computation.1 | async-start | bytes 6291456 | tf_op jit(solution)/shard_map/all_to_all | solution.py:421
  45.0 27.5 %collective-permute-start.1 = (bf16[8,2,256,128]{3,2,1,0:T(8,128)(2,1)}, bf16[8,2,256,128]{3,2,1,0:T(8,128)(2,1)S(1)}, u32[]{:S(2)}, u32[]{:S(2)}) collective-permute-start(bf16[8,2,256,128]{3,2,1,0:T(8,128)(2,1)} %slice.12), channel_id=1, source_target_pairs={{0,8},{1,9},{2,10},{3,11},{4,12},{5,13},{6,14},{7,15},{8,16},{9,17... | collective-permute-start | bytes 3145736 | tf_op jit(solution)/shard_map/ppermute | solution.py:428
  72.6 33.7 %collective-permute-start.2 = (bf16[8,2,256,128]{3,2,1,0:T(8,128)(2,1)S(1)}, bf16[8,2,256,128]{3,2,1,0:T(8,128)(2,1)}, u32[]{:S(2)}, u32[]{:S(2)}) collective-permute-start(bf16[8,2,256,128]{3,2,1,0:T(8,128)(2,1)S(1)} %collective-permute-done.1.refs_4_), channel_id=1, source_target_pairs={{0,8},{1,9},{2,10},{3,11},{4,12},{5,13},{6,14},{7,15},{8,16},{9,17... | collective-permute-start | bytes 3145736 | tf_op jit(solution)/shard_map/ppermute | solution.py:428
  74.8 31.2 %collective-permute-start.3 = (bf16[2,512,128]{2,1,0:T(8,128)(2,1)}, bf16[2,512,128]{2,1,0:T(8,128)(2,1)S(1)}, u32[]{:S(2)}, u32[]{:S(2)}) collective-permute-start(bf16[2,512,128]{2,1,0:T(8,128)(2,1)} %constant_dynamic-slice_fusion), channel_id=1, source_target_pairs={{0,24},{1,25},{2,26},{3,27},{4,28},{5,29},{6,30},{7,31}} | collective-permute-start | bytes 786440 | tf_op jit(solution)/shard_map/ppermute | solution.py:428
  91.1 44.7 %collective-permute-start.4 = (bf16[8,2,256,128]{3,2,1,0:T(8,128)(2,1)}, bf16[8,2,256,128]{3,2,1,0:T(8,128)(2,1)}, u32[]{:S(2)}, u32[]{:S(2)}) collective-permute-start(bf16[8,2,256,128]{3,2,1,0:T(8,128)(2,1)} %slice.11), channel_id=1, source_target_pairs={{0,8},{1,9},{2,10},{3,11},{4,12},{5,13},{6,14},{7,15},{8,16},{9,17... | collective-permute-start | bytes 3145736 | tf_op jit(solution)/shard_map/ppermute | solution.py:428
  118.7 27.3 %all-to-all-start.2 = ((bf16[8,2,256,128]{3,2,1,0:T(8,128)(2,1)}), bf16[8,2,256,128]{3,2,1,0:T(8,128)(2,1)S(1)}, u32[]{:S(2)}, u32[]{:S(2)}) async-start(bf16[8,2,256,128]{3,2,1,0:T(8,128)(2,1)} %shard_map.59), calls=%async_computation.2 | async-start | bytes 2097152 | tf_op jit(solution)/shard_map/all_to_all | solution.py:421
where the time goes:
time: 169 us; the launch traced here: 168 us
  Pallas kernels  76.1 us (45%)
  waiting for transfers between devices  46.9 us (28%)
  blocking collectives  19.4 us (11%)
  starting transfers between devices  18.8 us (11%)
  local copies, waits for them, and re-layouts  6.19 us (4%)
    pallas_call x6, Pallas kernels, attend(): pl.pallas_call(functools.partial(attend_kernel, step=step, steerable=bias...  66.8 us
    all_to_all x3, waiting for transfers between devices, exchange(): lax.all_to_all(blocks, 'seq', split_axis=0, concat_axis=0, axis_index_gro...  25.4 us
    ppermute x5, waiting for transfers between devices, onward(): return lax.ppermute(blocks, 'seq', pairs)  21.5 us
    all_to_all x1, blocking collectives, exchange(): lax.all_to_all(blocks, 'seq', split_axis=0, concat_axis=0, axis_index_gro...  19.4 us
    all_to_all x3, starting transfers between devices, exchange(): lax.all_to_all(blocks, 'seq', split_axis=0, concat_axis=0, axis_index_gro...  12.2 us
    ppermute x5, starting transfers between devices, onward(): return lax.ppermute(blocks, 'seq', pairs)  6.59 us
    pallas_call x1, Pallas kernels, pack(): pl.pallas_call(pack_kernel, grid=(TOKEN_STEPS,), in_specs=[smem()] * 3 +...  6.5 us
  transfers between devices with their start and end apart: 8, of which 4 were waited for; matrix products, arithmetic and copies ran while one was open for 3% of the time, Pallas kernels for 40%

commit v1 on v0

--- a/solution.py
+++ b/solution.py
@@ -379,7 +379,7 @@
         scratch_shapes=scratch,
         compiler_params=params(),
         cost_estimate=cost(
-            pair * (blocks * rows) ** 2 / (1 if step == 1 else 2),
+            pair * (blocks * rows) ** 2 * (16 if step == 1 and bias is not None else 1) / 2,
             8 * queries.size + 8 * pair * blocks * rows * width,
         ),
     )(*operands)
@@ -443,9 +443,9 @@
     both_a = exchange(both_a)
     states_a = both_a[:, :2]
     back_a = onward(after(states_a, raw_b))
-    all_b = lax.dynamic_update_slice(all_b, after(raw_b, states_a), (0, 0, 0, 0))
+    held_a = attend(0, scalars, bias, after(both_a, raw_b), both_a)
+    all_b = lax.dynamic_update_slice(all_b, after(raw_b, held_a), (0, 0, 0, 0))
     all_b = exchange(all_b)
-    held_a = attend(0, scalars, bias, after(both_a, raw_b), both_a)
     far_a = onward(after(back_a, held_a))
     length = GROUP * rows
     span_states = lax.dynamic_slice_in_dim(

time: 169 us -> 173 us (1.024)
  the two profiles are of different devices: /device:TPU:24 before, /device:TPU:16 now
where the time goes in v1:
time: 173 us; the launch traced here: 172 us
  Pallas kernels  76.1 us (44%)
  waiting for transfers between devices  42.7 us (25%)
  starting transfers between devices  25.7 us (15%)
  blocking collectives  19.3 us (11%)
  local copies, waits for them, and re-layouts  7.54 us (4%)
    pallas_call x6, Pallas kernels, attend(): pl.pallas_call(functools.partial(attend_kernel, step=step, steerable=bias...  66.8 us
    all_to_all x3, waiting for transfers between devices, exchange(): lax.all_to_all(blocks, 'seq', split_axis=0, concat_axis=0, axis_index_gro...  35.1 us
    all_to_all x1, blocking collectives, exchange(): lax.all_to_all(blocks, 'seq', split_axis=0, concat_axis=0, axis_index_gro...  19.3 us
    ppermute x5, starting transfers between devices, onward(): return lax.ppermute(blocks, 'seq', pairs)  13.8 us
    all_to_all x3, starting transfers between devices, exchange(): lax.all_to_all(blocks, 'seq', split_axis=0, concat_axis=0, axis_index_gro...  11.9 us
    ppermute x5, waiting for transfers between devices, onward(): return lax.ppermute(blocks, 'seq', pairs)  7.65 us
    pallas_call x1, Pallas kernels, pack(): pl.pallas_call(pack_kernel, grid=(TOKEN_STEPS,), in_specs=[smem()] * 3 +...  6.49 us
  transfers between devices with their start and end apart: 8, of which 3 were waited for; matrix products, arithmetic and copies ran while one was open for 4% of the time, Pallas kernels for 39%

profile of v1, /device:TPU:16, one launch (start us, length us, event | category | flops | bytes accessed | tf_op | source)
XLA Modules:
  0.0 172.1 jit_solution(457650756514183527)
XLA Ops:
  0.7 0.0 copy-start
  0.7 0.6 copy-done
  1.3 6.5 %shard_map.55 = (bf16[8,4,256,128]{3,2,1,0:T(8,128)(2,1)}, bf16[8,2,256,128]{3,2,1,0:T(8,128)(2,1)}, bf16[8,6,256,128]{3,2,1,0:T(8,128)(2,1)}, s32[36]{0:T(128)S(1)}) custom-call(s32[1]{0:T(128)} %bitcast.index_ref, s32[1]{0:T(128)} %copy.8.span_ref, s32[8]{0:T(128)S(1)} %copy-done, bf16[256,32,128]{2,1,0:T(8,128)(2,1)} %queries_ref.1, ...), custom_call_target="tpu_custom_call" | custom-call | bytes 8388608 | tf_op jit(solution)/shard_map/pallas_call | solution.py:108
  7.8 0.0 copy-start.2
  7.8 3.9 %all-to-all-start = ((bf16[8,4,256,128]{3,2,1,0:T(8,128)(2,1)}), bf16[8,4,256,128]{3,2,1,0:T(8,128)(2,1)S(1)}, u32[]{:S(2)}, u32[]{:S(2)}) async-start(bf16[8,4,256,128]{3,2,1,0:T(8,128)(2,1)} %get-tuple-element.28), calls=%async_computation | async-start | bytes 4194304 | tf_op jit(solution)/shard_map/all_to_all | solution.py:421
  11.7 0.0 copy-start.1
  11.7 0.0 copy-done.2
  11.7 3.5 %collective-permute-start = (bf16[8,2,256,128]{3,2,1,0:T(8,128)(2,1)S(1)}, bf16[8,2,256,128]{3,2,1,0:T(8,128)(2,1)}, u32[]{:S(2)}, u32[]{:S(2)}) collective-permute-start(bf16[8,2,256,128]{3,2,1,0:T(8,128)(2,1)S(1)} %copy-done.2), channel_id=1, source_target_pairs={{0,8},{1,9},{2,10},{3,11},{4,12},{5,13},{6,14},{7,15},{8,16},{9,17... | collective-permute-start | bytes 3145736 | tf_op jit(solution)/shard_map/ppermute | solution.py:428
  15.2 23.1 %all-to-all-done.refs_2_.refs_3_.refs_4_ = bf16[8,4,256,128]{3,2,1,0:T(8,128)(2,1)S(1)} async-done(((bf16[8,4,256,128]{3,2,1,0:T(8,128)(2,1)}), bf16[8,4,256,128]{3,2,1,0:T(8,128)(2,1)S(1)}, u32[]{:S(2)}, u32[]{:S(2)}) %all-to-all-start) | async-done | bytes 2097184 | tf_op jit(solution)/shard_map/all_to_all | solution.py:421
  38.3 1.2 slice.12
  39.5 0.0 collective-permute-done
  39.5 3.5 %collective-permute-start.1 = (bf16[8,2,256,128]{3,2,1,0:T(8,128)(2,1)}, bf16[8,2,256,128]{3,2,1,0:T(8,128)(2,1)S(1)}, u32[]{:S(2)}, u32[]{:S(2)}) collective-permute-start(bf16[8,2,256,128]{3,2,1,0:T(8,128)(2,1)} %slice.12), channel_id=1, source_target_pairs={{0,8},{1,9},{2,10},{3,11},{4,12},{5,13},{6,14},{7,15},{8,16},{9,17... | collective-permute-start | bytes 3145736 | tf_op jit(solution)/shard_map/ppermute | solution.py:428
  42.9 0.0 copy-done.1
  43.0 8.8 %shard_map.56 = (f32[4,2,512,128]{3,2,1,0:T(8,128)}, f32[4,2,512,128]{3,2,1,0:T(8,128)}) custom-call(s32[36]{0:T(128)S(1)} %get-tuple-element.27.refs_0_.scalars, f32[32,256]{1,0:T(8,128)S(1)} %reshape.10.refs_1_, bf16[8,4,256,128]{3,2,1,0:T(8,128)(2,1)S(1)} %all-to-all-done.refs_2_.refs_3_.refs_4_, ...), custom_call_target="tpu_custom_call" | custom-call | flops 1073741824 | bytes 12582912 | tf_op jit(solution)/shard_map/pallas_call | solution.py:373
  51.8 2.4 %constant_dynamic-update-slice_fusion = bf16[8,6,256,128]{3,2,1,0:T(8,128)(2,1)} fusion(bf16[8,6,256,128]{3,2,1,0:T(8,128)(2,1)} %get-tuple-element.38, bf16[8,2,256,128]{3,2,1,0:T(8,128)(2,1)} %collective-permute-done), kind=kLoop, calls=%fused_computation.5 | loop fusion | bytes 2097152 | tf_op jit(solution)/shard_map/dynamic_update_slice | solution.py:447
  54.3 4.5 %all-to-all-start.1 = ((bf16[8,6,256,128]{3,2,1,0:T(8,128)(2,1)}), bf16[8,6,256,128]{3,2,1,0:T(8,128)(2,1)}, u32[]{:S(2)}, u32[]{:S(2)}) async-start(bf16[8,6,256,128]{3,2,1,0:T(8,128)(2,1)} %constant_dynamic-update-slice_fusion), calls=%async_computation.1 | async-start | bytes 6291456 | tf_op jit(solution)/shard_map/all_to_all | solution.py:421
  58.7 7.6 %collective-permute-done.1.refs_4_ = bf16[8,2,256,128]{3,2,1,0:T(8,128)(2,1)S(1)} collective-permute-done((bf16[8,2,256,128]{3,2,1,0:T(8,128)(2,1)}, bf16[8,2,256,128]{3,2,1,0:T(8,128)(2,1)S(1)}, u32[]{:S(2)}, u32[]{:S(2)}) %collective-permute-start.1) | collective-permute-done | bytes 1048608 | tf_op jit(solution)/shard_map/ppermute | solution.py:428
  66.4 0.1 slice_bitcast_fusion
  66.4 0.1 copy.6
  66.5 0.8 constant_dynamic-slice_fusion
  67.3 0.7 collective-permute-start.3
  68.0 4.1 %collective-permute-start.2 = (bf16[8,2,256,128]{3,2,1,0:T(8,128)(2,1)S(1)}, bf16[8,2,256,128]{3,2,1,0:T(8,128)(2,1)}, u32[]{:S(2)}, u32[]{:S(2)}) collective-permute-start(bf16[8,2,256,128]{3,2,1,0:T(8,128)(2,1)S(1)} %collective-permute-done.1.refs_4_), channel_id=1, source_target_pairs={{0,8},{1,9},{2,10},{3,11},{4,12},{5,13},{6,14},{7,15},{8,16},{9,17... | collective-permute-start | bytes 3145736 | tf_op jit(solution)/shard_map/ppermute | solution.py:428
  72.1 12.6 %shard_map.57 = (f32[4,2,512,128]{3,2,1,0:T(8,128)}, f32[4,2,512,128]{3,2,1,0:T(8,128)}) custom-call(s32[36]{0:T(128)S(1)} %get-tuple-element.27.refs_0_.scalars, f32[32,256]{1,0:T(8,128)S(1)} %reshape.10.refs_1_, bf16[8,4,256,128]{3,2,1,0:T(8,128)(2,1)S(1)} %all-to-all-done.refs_2_.refs_3_.refs_4_, ...), custom_call_target="tpu_custom_call" | custom-call | flops 17179869184 | bytes 12582912 | tf_op jit(solution)/shard_map/pallas_call | solution.py:373
  84.7 11.9 %all-to-all-done.1.refs_1_.refs_2_.refs_3_ = bf16[8,6,256,128]{3,2,1,0:T(8,128)(2,1)} async-done(((bf16[8,6,256,128]{3,2,1,0:T(8,128)(2,1)}), bf16[8,6,256,128]{3,2,1,0:T(8,128)(2,1)}, u32[]{:S(2)}, u32[]{:S(2)}) %all-to-all-start.1) | async-done | bytes 3145760 | tf_op jit(solution)/shard_map/all_to_all | solution.py:421
  96.6 2.3 %slice.11 = bf16[8,2,256,128]{3,2,1,0:T(8,128)(2,1)} slice(bf16[8,6,256,128]{3,2,1,0:T(8,128)(2,1)} %all-to-all-done.1.refs_1_.refs_2_.refs_3_), slice={[0:8], [0:2], [0:256], [0:128]} | slice | bytes 2097152 | tf_op jit(solution)/shard_map/slice | solution.py:460
  99.0 2.1 %collective-permute-start.4 = (bf16[8,2,256,128]{3,2,1,0:T(8,128)(2,1)}, bf16[8,2,256,128]{3,2,1,0:T(8,128)(2,1)}, u32[]{:S(2)}, u32[]{:S(2)}) collective-permute-start(bf16[8,2,256,128]{3,2,1,0:T(8,128)(2,1)} %slice.11), channel_id=1, source_target_pairs={{0,8},{1,9},{2,10},{3,11},{4,12},{5,13},{6,14},{7,15},{8,16},{9,17... | collective-permute-start | bytes 3145736 | tf_op jit(solution)/shard_map/ppermute | solution.py:428
  101.1 9.5 %shard_map.58 = (f32[4,2,512,128]{3,2,1,0:T(8,128)}, f32[4,2,512,128]{3,2,1,0:T(8,128)}) custom-call(s32[36]{0:T(128)S(1)} %get-tuple-element.27.refs_0_.scalars, bf16[8,6,256,128]{3,2,1,0:T(8,128)(2,1)} %all-to-all-done.1.refs_1_.refs_2_.refs_3_, bf16[8,6,256,128]{3,2,1,0:T(8,128)(2,1)} %all-to-all-done.1.refs_1_.refs_2_.refs_3_, ...), custom_call_target="tpu_custom_call" | custom-call | flops 1073741824 | bytes 16777216 | tf_op jit(solution)/shard_map/pallas_call | solution.py:373
  110.6 0.0 collective-permute-done.3.refs_5_
  110.6 0.0 collective-permute-done.2.refs_4_
  110.6 12.5 %shard_map.59 = bf16[8,2,256,128]{3,2,1,0:T(8,128)(2,1)} custom-call(s32[36]{0:T(128)S(1)} %get-tuple-element.27.refs_0_.scalars, f32[32,256]{1,0:T(8,128)S(1)} %reshape.10.refs_1_, bf16[8,4,256,128]{3,2,1,0:T(8,128)(2,1)S(1)} %all-to-all-done.refs_2_.refs_3_.refs_4_, bf16[8,4,256,128]{3,2,1,0:T(8,128)(2,1)S(1)} %all-to-all-done.refs_2_.refs_3_.refs_4_, ...), custom_call_target="tpu_custom_call" | custom-call | flops 1073741824 | bytes 12582912 | tf_op jit(solution)/shard_map/pallas_call | solution.py:373
  123.1 3.6 %all-to-all-start.2 = ((bf16[8,2,256,128]{3,2,1,0:T(8,128)(2,1)}), bf16[8,2,256,128]{3,2,1,0:T(8,128)(2,1)S(1)}, u32[]{:S(2)}, u32[]{:S(2)}) async-start(bf16[8,2,256,128]{3,2,1,0:T(8,128)(2,1)} %shard_map.59), calls=%async_computation.2 | async-start | bytes 2097152 | tf_op jit(solution)/shard_map/all_to_all | solution.py:421
  126.6 13.1 %shard_map.60 = (f32[4,2,512,128]{3,2,1,0:T(8,128)}, f32[4,2,512,128]{3,2,1,0:T(8,128)}) custom-call(s32[36]{0:T(128)S(1)} %get-tuple-element.27.refs_0_.scalars, bf16[8,6,256,128]{3,2,1,0:T(8,128)(2,1)} %all-to-all-done.1.refs_1_.refs_2_.refs_3_, bf16[8,6,256,128]{3,2,1,0:T(8,128)(2,1)} %all-to-all-done.1.refs_1_.refs_2_.refs_3_, ...), custom_call_target="tpu_custom_call" | custom-call | flops 1073741824 | bytes 16777216 | tf_op jit(solution)/shard_map/pallas_call | solution.py:373
  139.8 0.0 collective-permute-done.4.refs_3_
  139.8 10.2 %shard_map.61 = bf16[8,2,256,128]{3,2,1,0:T(8,128)(2,1)S(1)} custom-call(s32[36]{0:T(128)S(1)} %get-tuple-element.27.refs_0_.scalars, bf16[8,6,256,128]{3,2,1,0:T(8,128)(2,1)} %all-to-all-done.1.refs_1_.refs_2_.refs_3_, bf16[8,6,256,128]{3,2,1,0:T(8,128)(2,1)} %all-to-all-done.1.refs_1_.refs_2_.refs_3_, ...), custom_call_target="tpu_custom_call" | custom-call | flops 1073741824 | bytes 16777216 | tf_op jit(solution)/shard_map/pallas_call | solution.py:373
  150.0 0.0 all-to-all-done.2.out_a
  150.0 19.3 %all_to_all.20.out_b = bf16[8,2,256,128]{3,2,1,0:T(8,128)(2,1)S(1)} all-to-all(bf16[8,2,256,128]{3,2,1,0:T(8,128)(2,1)S(1)} %shard_map.61), channel_id=1, replica_groups={{0,1,2,3,4,5,6,7},{8,9,10,11,12,13,14,15},{16,17,18,19,20,21,22,23},{24..., dimensions={0} | all-to-all | bytes 2097152 | tf_op jit(solution)/shard_map/all_to_all | solution.py:421
  169.3 2.8 %shard_map.62 = bf16[256,32,128]{2,1,0:T(8,128)(2,1)} custom-call(s32[36]{0:T(128)S(1)} %get-tuple-element.27.refs_0_.scalars, bf16[8,2,256,128]{3,2,1,0:T(8,128)(2,1)S(1)} %all-to-all-done.2.out_a, bf16[8,2,256,128]{3,2,1,0:T(8,128)(2,1)S(1)} %all_to_all.20.out_b), custom_call_target="tpu_custom_call" | custom-call | bytes 4194304 | tf_op jit(solution)/shard_map/pallas_call | solution.py:399
  (2 shorter events, 0.0 us)
Async XLA Ops:
  0.7 0.7 copy-start
  7.8 3.9 %copy-start.2 = (bf16[8,2,256,128]{3,2,1,0:T(8,128)(2,1)S(1)}, bf16[8,2,256,128]{3,2,1,0:T(8,128)(2,1)}, u32[]{:S(2)}) copy-start(bf16[8,2,256,128]{3,2,1,0:T(8,128)(2,1)} %get-tuple-element.29) | copy-start | bytes 3145732
  7.8 30.5 %all-to-all-start = ((bf16[8,4,256,128]{3,2,1,0:T(8,128)(2,1)}), bf16[8,4,256,128]{3,2,1,0:T(8,128)(2,1)S(1)}, u32[]{:S(2)}, u32[]{:S(2)}) async-start(bf16[8,4,256,128]{3,2,1,0:T(8,128)(2,1)} %get-tuple-element.28), calls=%async_computation | async-start | bytes 4194304 | tf_op jit(solution)/shard_map/all_to_all | solution.py:421
  11.7 31.3 %copy-start.1 = (bf16[8192]{0:T(1024)(128)(2,1)S(1)}, bf16[8192]{0:T(1024)(128)(2,1)}, u32[]{:S(2)}) copy-start(bf16[8192]{0:T(1024)(128)(2,1)} %param.7) | copy-start | bytes 49156
  11.7 27.8 %collective-permute-start = (bf16[8,2,256,128]{3,2,1,0:T(8,128)(2,1)S(1)}, bf16[8,2,256,128]{3,2,1,0:T(8,128)(2,1)}, u32[]{:S(2)}, u32[]{:S(2)}) collective-permute-start(bf16[8,2,256,128]{3,2,1,0:T(8,128)(2,1)S(1)} %copy-done.2), channel_id=1, source_target_pairs={{0,8},{1,9},{2,10},{3,11},{4,12},{5,13},{6,14},{7,15},{8,16},{9,17... | collective-permute-start | bytes 3145736 | tf_op jit(solution)/shard_map/ppermute | solution.py:428
  39.5 26.9 %collective-permute-start.1 = (bf16[8,2,256,128]{3,2,1,0:T(8,128)(2,1)}, bf16[8,2,256,128]{3,2,1,0:T(8,128)(2,1)S(1)}, u32[]{:S(2)}, u32[]{:S(2)}) collective-permute-start(bf16[8,2,256,128]{3,2,1,0:T(8,128)(2,1)} %slice.12), channel_id=1, source_target_pairs={{0,8},{1,9},{2,10},{3,11},{4,12},{5,13},{6,14},{7,15},{8,16},{9,17... | collective-permute-start | bytes 3145736 | tf_op jit(solution)/shard_map/ppermute | solution.py:428
  54.3 42.3 %all-to-all-start.1 = ((bf16[8,6,256,128]{3,2,1,0:T(8,128)(2,1)}), bf16[8,6,256,128]{3,2,1,0:T(8,128)(2,1)}, u32[]{:S(2)}, u32[]{:S(2)}) async-start(bf16[8,6,256,128]{3,2,1,0:T(8,128)(2,1)} %constant_dynamic-update-slice_fusion), calls=%async_computation.1 | async-start | bytes 6291456 | tf_op jit(solution)/shard_map/all_to_all | solution.py:421
  67.3 43.3 %collective-permute-start.3 = (bf16[2,512,128]{2,1,0:T(8,128)(2,1)}, bf16[2,512,128]{2,1,0:T(8,128)(2,1)S(1)}, u32[]{:S(2)}, u32[]{:S(2)}) collective-permute-start(bf16[2,512,128]{2,1,0:T(8,128)(2,1)} %constant_dynamic-slice_fusion), channel_id=1, source_target_pairs={{0,24},{1,25},{2,26},{3,27},{4,28},{5,29},{6,30},{7,31}} | collective-permute-start | bytes 786440 | tf_op jit(solution)/shard_map/ppermute | solution.py:428
  68.0 42.6 %collective-permute-start.2 = (bf16[8,2,256,128]{3,2,1,0:T(8,128)(2,1)S(1)}, bf16[8,2,256,128]{3,2,1,0:T(8,128)(2,1)}, u32[]{:S(2)}, u32[]{:S(2)}) collective-permute-start(bf16[8,2,256,128]{3,2,1,0:T(8,128)(2,1)S(1)} %collective-permute-done.1.refs_4_), channel_id=1, source_target_pairs={{0,8},{1,9},{2,10},{3,11},{4,12},{5,13},{6,14},{7,15},{8,16},{9,17... | collective-permute-start | bytes 3145736 | tf_op jit(solution)/shard_map/ppermute | solution.py:428
  99.0 40.8 %collective-permute-start.4 = (bf16[8,2,256,128]{3,2,1,0:T(8,128)(2,1)}, bf16[8,2,256,128]{3,2,1,0:T(8,128)(2,1)}, u32[]{:S(2)}, u32[]{:S(2)}) collective-permute-start(bf16[8,2,256,128]{3,2,1,0:T(8,128)(2,1)} %slice.11), channel_id=1, source_target_pairs={{0,8},{1,9},{2,10},{3,11},{4,12},{5,13},{6,14},{7,15},{8,16},{9,17... | collective-permute-start | bytes 3145736 | tf_op jit(solution)/shard_map/ppermute | solution.py:428
  123.1 26.9 %all-to-all-start.2 = ((bf16[8,2,256,128]{3,2,1,0:T(8,128)(2,1)}), bf16[8,2,256,128]{3,2,1,0:T(8,128)(2,1)S(1)}, u32[]{:S(2)}, u32[]{:S(2)}) async-start(bf16[8,2,256,128]{3,2,1,0:T(8,128)(2,1)} %shard_map.59), calls=%async_computation.2 | async-start | bytes 2097152 | tf_op jit(solution)/shard_map/all_to_all | solution.py:421

commit v2 on v1

--- a/solution.py
+++ b/solution.py
@@ -444,7 +444,7 @@
     states_a = both_a[:, :2]
     back_a = onward(after(states_a, raw_b))
     held_a = attend(0, scalars, bias, after(both_a, raw_b), both_a)
-    all_b = lax.dynamic_update_slice(all_b, after(raw_b, held_a), (0, 0, 0, 0))
+    all_b = lax.dynamic_update_slice(all_b, after(raw_b, states_a), (0, 0, 0, 0))
     all_b = exchange(all_b)
     far_a = onward(after(back_a, held_a))
     length = GROUP * rows

time: 173 us -> 164 us (0.948)
  the two profiles are of different devices: /device:TPU:16 before, /device:TPU:24 now
where the time goes in v2:
time: 164 us; the launch traced here: 162 us
  Pallas kernels  76.1 us (46%)
  waiting for transfers between devices  39.9 us (24%)
  blocking collectives  19.3 us (12%)
  starting transfers between devices  18.6 us (11%)
  local copies, waits for them, and re-layouts  7.47 us (5%)
    pallas_call x6, Pallas kernels, attend(): pl.pallas_call(functools.partial(attend_kernel, step=step, steerable=bias...  66.8 us
    all_to_all x3, waiting for transfers between devices, exchange(): lax.all_to_all(blocks, 'seq', split_axis=0, concat_axis=0, axis_index_gro...  28.6 us
    all_to_all x1, blocking collectives, exchange(): lax.all_to_all(blocks, 'seq', split_axis=0, concat_axis=0, axis_index_gro...  19.3 us
    all_to_all x3, starting transfers between devices, exchange(): lax.all_to_all(blocks, 'seq', split_axis=0, concat_axis=0, axis_index_gro...  12 us
    ppermute x5, waiting for transfers between devices, onward(): return lax.ppermute(blocks, 'seq', pairs)  11.3 us
    ppermute x5, starting transfers between devices, onward(): return lax.ppermute(blocks, 'seq', pairs)  6.61 us
    pallas_call x1, Pallas kernels, pack(): pl.pallas_call(pack_kernel, grid=(TOKEN_STEPS,), in_specs=[smem()] * 3 +...  6.49 us
  transfers between devices with their start and end apart: 8, of which 4 were waited for; matrix products, arithmetic and copies ran while one was open for 4% of the time, Pallas kernels for 41%

profile of v2, /device:TPU:24, one launch (start us, length us, event | category | flops | bytes accessed | tf_op | source)
XLA Modules:
  0.0 162.2 jit_solution(3855644052965331147)
XLA Ops:
  0.7 0.0 copy-start
  0.7 0.6 copy-done
  1.3 6.5 %shard_map.55 = (bf16[8,4,256,128]{3,2,1,0:T(8,128)(2,1)}, bf16[8,2,256,128]{3,2,1,0:T(8,128)(2,1)}, bf16[8,6,256,128]{3,2,1,0:T(8,128)(2,1)}, s32[36]{0:T(128)S(1)}) custom-call(s32[1]{0:T(128)} %bitcast.index_ref, s32[1]{0:T(128)} %copy.8.span_ref, s32[8]{0:T(128)S(1)} %copy-done, bf16[256,32,128]{2,1,0:T(8,128)(2,1)} %queries_ref.1, ...), custom_call_target="tpu_custom_call" | custom-call | bytes 8388608 | tf_op jit(solution)/shard_map/pallas_call | solution.py:108
  7.8 0.0 copy-start.2
  7.8 3.9 %all-to-all-start = ((bf16[8,4,256,128]{3,2,1,0:T(8,128)(2,1)}), bf16[8,4,256,128]{3,2,1,0:T(8,128)(2,1)S(1)}, u32[]{:S(2)}, u32[]{:S(2)}) async-start(bf16[8,4,256,128]{3,2,1,0:T(8,128)(2,1)} %get-tuple-element.28), calls=%async_computation | async-start | bytes 4194304 | tf_op jit(solution)/shard_map/all_to_all | solution.py:421
  11.7 0.0 copy-done.2
  11.7 1.3 collective-permute-start
  13.0 25.3 %all-to-all-done.refs_2_.refs_3_.refs_4_ = bf16[8,4,256,128]{3,2,1,0:T(8,128)(2,1)S(1)} async-done(((bf16[8,4,256,128]{3,2,1,0:T(8,128)(2,1)}), bf16[8,4,256,128]{3,2,1,0:T(8,128)(2,1)S(1)}, u32[]{:S(2)}, u32[]{:S(2)}) %all-to-all-start) | async-done | bytes 2097184 | tf_op jit(solution)/shard_map/all_to_all | solution.py:421
  38.3 1.1 slice.12
  39.4 0.0 collective-permute-done
  39.4 1.3 collective-permute-start.1
  40.6 2.4 %constant_dynamic-update-slice_fusion = bf16[8,6,256,128]{3,2,1,0:T(8,128)(2,1)} fusion(bf16[8,6,256,128]{3,2,1,0:T(8,128)(2,1)} %get-tuple-element.38, bf16[8,2,256,128]{3,2,1,0:T(8,128)(2,1)} %collective-permute-done), kind=kLoop, calls=%fused_computation.5 | loop fusion | bytes 2097152 | tf_op jit(solution)/shard_map/dynamic_update_slice | solution.py:447
  43.1 0.0 copy-start.1
  43.1 4.6 %all-to-all-start.1 = ((bf16[8,6,256,128]{3,2,1,0:T(8,128)(2,1)}), bf16[8,6,256,128]{3,2,1,0:T(8,128)(2,1)}, u32[]{:S(2)}, u32[]{:S(2)}) async-start(bf16[8,6,256,128]{3,2,1,0:T(8,128)(2,1)} %constant_dynamic-update-slice_fusion), calls=%async_computation.1 | async-start | bytes 6291456 | tf_op jit(solution)/shard_map/all_to_all | solution.py:421
  47.7 0.0 copy-done.1
  47.8 8.8 %shard_map.56 = (f32[4,2,512,128]{3,2,1,0:T(8,128)}, f32[4,2,512,128]{3,2,1,0:T(8,128)}) custom-call(s32[36]{0:T(128)S(1)} %get-tuple-element.27.refs_0_.scalars, f32[32,256]{1,0:T(8,128)S(1)} %reshape.10.refs_1_, bf16[8,4,256,128]{3,2,1,0:T(8,128)(2,1)S(1)} %all-to-all-done.refs_2_.refs_3_.refs_4_, ...), custom_call_target="tpu_custom_call" | custom-call | flops 1073741824 | bytes 12582912 | tf_op jit(solution)/shard_map/pallas_call | solution.py:373
  56.6 9.5 %collective-permute-done.1.refs_4_ = bf16[8,2,256,128]{3,2,1,0:T(8,128)(2,1)S(1)} collective-permute-done((bf16[8,2,256,128]{3,2,1,0:T(8,128)(2,1)}, bf16[8,2,256,128]{3,2,1,0:T(8,128)(2,1)S(1)}, u32[]{:S(2)}, u32[]{:S(2)}) %collective-permute-start.1) | collective-permute-done | bytes 1048608 | tf_op jit(solution)/shard_map/ppermute | solution.py:428
  66.1 0.1 slice_bitcast_fusion
  66.2 0.1 copy.6
  66.3 0.8 constant_dynamic-slice_fusion
  67.1 1.3 collective-permute-start.3
  68.4 1.3 collective-permute-start.2
  69.7 12.6 %shard_map.57 = (f32[4,2,512,128]{3,2,1,0:T(8,128)}, f32[4,2,512,128]{3,2,1,0:T(8,128)}) custom-call(s32[36]{0:T(128)S(1)} %get-tuple-element.27.refs_0_.scalars, f32[32,256]{1,0:T(8,128)S(1)} %reshape.10.refs_1_, bf16[8,4,256,128]{3,2,1,0:T(8,128)(2,1)S(1)} %all-to-all-done.refs_2_.refs_3_.refs_4_, ...), custom_call_target="tpu_custom_call" | custom-call | flops 17179869184 | bytes 12582912 | tf_op jit(solution)/shard_map/pallas_call | solution.py:373
  82.3 3.3 %all-to-all-done.1.refs_1_.refs_2_.refs_3_ = bf16[8,6,256,128]{3,2,1,0:T(8,128)(2,1)} async-done(((bf16[8,6,256,128]{3,2,1,0:T(8,128)(2,1)}), bf16[8,6,256,128]{3,2,1,0:T(8,128)(2,1)}, u32[]{:S(2)}, u32[]{:S(2)}) %all-to-all-start.1) | async-done | bytes 3145760 | tf_op jit(solution)/shard_map/all_to_all | solution.py:421
  85.6 2.3 %slice.11 = bf16[8,2,256,128]{3,2,1,0:T(8,128)(2,1)} slice(bf16[8,6,256,128]{3,2,1,0:T(8,128)(2,1)} %all-to-all-done.1.refs_1_.refs_2_.refs_3_), slice={[0:8], [0:2], [0:256], [0:128]} | slice | bytes 2097152 | tf_op jit(solution)/shard_map/slice | solution.py:460
  87.9 1.5 collective-permute-start.4
  89.4 9.5 %shard_map.58 = (f32[4,2,512,128]{3,2,1,0:T(8,128)}, f32[4,2,512,128]{3,2,1,0:T(8,128)}) custom-call(s32[36]{0:T(128)S(1)} %get-tuple-element.27.refs_0_.scalars, bf16[8,6,256,128]{3,2,1,0:T(8,128)(2,1)} %all-to-all-done.1.refs_1_.refs_2_.refs_3_, bf16[8,6,256,128]{3,2,1,0:T(8,128)(2,1)} %all-to-all-done.1.refs_1_.refs_2_.refs_3_, ...), custom_call_target="tpu_custom_call" | custom-call | flops 1073741824 | bytes 16777216 | tf_op jit(solution)/shard_map/pallas_call | solution.py:373
  98.9 0.0 collective-permute-done.3.refs_5_
  98.9 1.8 %collective-permute-done.2.refs_4_ = bf16[8,2,256,128]{3,2,1,0:T(8,128)(2,1)} collective-permute-done((bf16[8,2,256,128]{3,2,1,0:T(8,128)(2,1)S(1)}, bf16[8,2,256,128]{3,2,1,0:T(8,128)(2,1)}, u32[]{:S(2)}, u32[]{:S(2)}) %collective-permute-start.2) | collective-permute-done | bytes 1048608 | tf_op jit(solution)/shard_map/ppermute | solution.py:428
  100.7 12.4 %shard_map.59 = bf16[8,2,256,128]{3,2,1,0:T(8,128)(2,1)} custom-call(s32[36]{0:T(128)S(1)} %get-tuple-element.27.refs_0_.scalars, f32[32,256]{1,0:T(8,128)S(1)} %reshape.10.refs_1_, bf16[8,4,256,128]{3,2,1,0:T(8,128)(2,1)S(1)} %all-to-all-done.refs_2_.refs_3_.refs_4_, bf16[8,4,256,128]{3,2,1,0:T(8,128)(2,1)S(1)} %all-to-all-done.refs_2_.refs_3_.refs_4_, ...), custom_call_target="tpu_custom_call" | custom-call | flops 1073741824 | bytes 12582912 | tf_op jit(solution)/shard_map/pallas_call | solution.py:373
  113.2 3.6 %all-to-all-start.2 = ((bf16[8,2,256,128]{3,2,1,0:T(8,128)(2,1)}), bf16[8,2,256,128]{3,2,1,0:T(8,128)(2,1)S(1)}, u32[]{:S(2)}, u32[]{:S(2)}) async-start(bf16[8,2,256,128]{3,2,1,0:T(8,128)(2,1)} %shard_map.59), calls=%async_computation.2 | async-start | bytes 2097152 | tf_op jit(solution)/shard_map/all_to_all | solution.py:421
  116.7 13.1 %shard_map.60 = (f32[4,2,512,128]{3,2,1,0:T(8,128)}, f32[4,2,512,128]{3,2,1,0:T(8,128)}) custom-call(s32[36]{0:T(128)S(1)} %get-tuple-element.27.refs_0_.scalars, bf16[8,6,256,128]{3,2,1,0:T(8,128)(2,1)} %all-to-all-done.1.refs_1_.refs_2_.refs_3_, bf16[8,6,256,128]{3,2,1,0:T(8,128)(2,1)} %all-to-all-done.1.refs_1_.refs_2_.refs_3_, ...), custom_call_target="tpu_custom_call" | custom-call | flops 1073741824 | bytes 16777216 | tf_op jit(solution)/shard_map/pallas_call | solution.py:373
  129.9 0.0 collective-permute-done.4.refs_3_
  129.9 10.2 %shard_map.61 = bf16[8,2,256,128]{3,2,1,0:T(8,128)(2,1)S(1)} custom-call(s32[36]{0:T(128)S(1)} %get-tuple-element.27.refs_0_.scalars, bf16[8,6,256,128]{3,2,1,0:T(8,128)(2,1)} %all-to-all-done.1.refs_1_.refs_2_.refs_3_, bf16[8,6,256,128]{3,2,1,0:T(8,128)(2,1)} %all-to-all-done.1.refs_1_.refs_2_.refs_3_, ...), custom_call_target="tpu_custom_call" | custom-call | flops 1073741824 | bytes 16777216 | tf_op jit(solution)/shard_map/pallas_call | solution.py:373
  140.1 0.0 all-to-all-done.2.out_a
  140.1 19.3 %all_to_all.20.out_b = bf16[8,2,256,128]{3,2,1,0:T(8,128)(2,1)S(1)} all-to-all(bf16[8,2,256,128]{3,2,1,0:T(8,128)(2,1)S(1)} %shard_map.61), channel_id=1, replica_groups={{0,1,2,3,4,5,6,7},{8,9,10,11,12,13,14,15},{16,17,18,19,20,21,22,23},{24..., dimensions={0} | all-to-all | bytes 2097152 | tf_op jit(solution)/shard_map/all_to_all | solution.py:421
  159.4 2.8 %shard_map.62 = bf16[256,32,128]{2,1,0:T(8,128)(2,1)} custom-call(s32[36]{0:T(128)S(1)} %get-tuple-element.27.refs_0_.scalars, bf16[8,2,256,128]{3,2,1,0:T(8,128)(2,1)S(1)} %all-to-all-done.2.out_a, bf16[8,2,256,128]{3,2,1,0:T(8,128)(2,1)S(1)} %all_to_all.20.out_b), custom_call_target="tpu_custom_call" | custom-call | bytes 4194304 | tf_op jit(solution)/shard_map/pallas_call | solution.py:399
  (2 shorter events, 0.0 us)
Async XLA Ops:
  0.7 0.7 copy-start
  7.8 3.9 %copy-start.2 = (bf16[8,2,256,128]{3,2,1,0:T(8,128)(2,1)S(1)}, bf16[8,2,256,128]{3,2,1,0:T(8,128)(2,1)}, u32[]{:S(2)}) copy-start(bf16[8,2,256,128]{3,2,1,0:T(8,128)(2,1)} %get-tuple-element.29) | copy-start | bytes 3145732
  7.8 30.5 %all-to-all-start = ((bf16[8,4,256,128]{3,2,1,0:T(8,128)(2,1)}), bf16[8,4,256,128]{3,2,1,0:T(8,128)(2,1)S(1)}, u32[]{:S(2)}, u32[]{:S(2)}) async-start(bf16[8,4,256,128]{3,2,1,0:T(8,128)(2,1)} %get-tuple-element.28), calls=%async_computation | async-start | bytes 4194304 | tf_op jit(solution)/shard_map/all_to_all | solution.py:421
  11.7 27.7 %collective-permute-start = (bf16[8,2,256,128]{3,2,1,0:T(8,128)(2,1)S(1)}, bf16[8,2,256,128]{3,2,1,0:T(8,128)(2,1)}, u32[]{:S(2)}, u32[]{:S(2)}) collective-permute-start(bf16[8,2,256,128]{3,2,1,0:T(8,128)(2,1)S(1)} %copy-done.2), channel_id=1, source_target_pairs={{0,8},{1,9},{2,10},{3,11},{4,12},{5,13},{6,14},{7,15},{8,16},{9,17... | collective-permute-start | bytes 3145736 | tf_op jit(solution)/shard_map/ppermute | solution.py:428
  39.4 26.7 %collective-permute-start.1 = (bf16[8,2,256,128]{3,2,1,0:T(8,128)(2,1)}, bf16[8,2,256,128]{3,2,1,0:T(8,128)(2,1)S(1)}, u32[]{:S(2)}, u32[]{:S(2)}) collective-permute-start(bf16[8,2,256,128]{3,2,1,0:T(8,128)(2,1)} %slice.12), channel_id=1, source_target_pairs={{0,8},{1,9},{2,10},{3,11},{4,12},{5,13},{6,14},{7,15},{8,16},{9,17... | collective-permute-start | bytes 3145736 | tf_op jit(solution)/shard_map/ppermute | solution.py:428
  43.1 4.6 %copy-start.1 = (bf16[8192]{0:T(1024)(128)(2,1)S(1)}, bf16[8192]{0:T(1024)(128)(2,1)}, u32[]{:S(2)}) copy-start(bf16[8192]{0:T(1024)(128)(2,1)} %param.7) | copy-start | bytes 49156
  43.1 42.5 %all-to-all-start.1 = ((bf16[8,6,256,128]{3,2,1,0:T(8,128)(2,1)}), bf16[8,6,256,128]{3,2,1,0:T(8,128)(2,1)}, u32[]{:S(2)}, u32[]{:S(2)}) async-start(bf16[8,6,256,128]{3,2,1,0:T(8,128)(2,1)} %constant_dynamic-update-slice_fusion), calls=%async_computation.1 | async-start | bytes 6291456 | tf_op jit(solution)/shard_map/all_to_all | solution.py:421
  67.1 31.8 %collective-permute-start.3 = (bf16[2,512,128]{2,1,0:T(8,128)(2,1)}, bf16[2,512,128]{2,1,0:T(8,128)(2,1)S(1)}, u32[]{:S(2)}, u32[]{:S(2)}) collective-permute-start(bf16[2,512,128]{2,1,0:T(8,128)(2,1)} %constant_dynamic-slice_fusion), channel_id=1, source_target_pairs={{0,24},{1,25},{2,26},{3,27},{4,28},{5,29},{6,30},{7,31}} | collective-permute-start | bytes 786440 | tf_op jit(solution)/shard_map/ppermute | solution.py:428
  68.4 32.4 %collective-permute-start.2 = (bf16[8,2,256,128]{3,2,1,0:T(8,128)(2,1)S(1)}, bf16[8,2,256,128]{3,2,1,0:T(8,128)(2,1)}, u32[]{:S(2)}, u32[]{:S(2)}) collective-permute-start(bf16[8,2,256,128]{3,2,1,0:T(8,128)(2,1)S(1)} %collective-permute-done.1.refs_4_), channel_id=1, source_target_pairs={{0,8},{1,9},{2,10},{3,11},{4,12},{5,13},{6,14},{7,15},{8,16},{9,17... | collective-permute-start | bytes 3145736 | tf_op jit(solution)/shard_map/ppermute | solution.py:428
  87.9 41.9 %collective-permute-start.4 = (bf16[8,2,256,128]{3,2,1,0:T(8,128)(2,1)}, bf16[8,2,256,128]{3,2,1,0:T(8,128)(2,1)}, u32[]{:S(2)}, u32[]{:S(2)}) collective-permute-start(bf16[8,2,256,128]{3,2,1,0:T(8,128)(2,1)} %slice.11), channel_id=1, source_target_pairs={{0,8},{1,9},{2,10},{3,11},{4,12},{5,13},{6,14},{7,15},{8,16},{9,17... | collective-permute-start | bytes 3145736 | tf_op jit(solution)/shard_map/ppermute | solution.py:428
  113.2 27.0 %all-to-all-start.2 = ((bf16[8,2,256,128]{3,2,1,0:T(8,128)(2,1)}), bf16[8,2,256,128]{3,2,1,0:T(8,128)(2,1)S(1)}, u32[]{:S(2)}, u32[]{:S(2)}) async-start(bf16[8,2,256,128]{3,2,1,0:T(8,128)(2,1)} %shard_map.59), calls=%async_computation.2 | async-start | bytes 2097152 | tf_op jit(solution)/shard_map/all_to_all | solution.py:421

commit v3 on v2

--- a/solution.py
+++ b/solution.py
@@ -143,11 +143,12 @@
     return sums
 
 
-def attend_kernel(*refs, step, steerable, last):
+def attend_kernel(*refs, step, steerable, last, joined):
     refs = list(refs)
     scalars = refs.pop(0)
     bias_ref = refs.pop(0) if steerable else None
     low_ref, high_ref, states_ref = refs.pop(0), refs.pop(0), refs.pop(0)
+    far_ref = refs.pop(0) if joined else None
     span_ref = refs.pop(0) if steerable and last else None
     if step:
         old_weighted, old_sums = refs.pop(0), refs.pop(0)
@@ -172,6 +173,8 @@
     flag_values = [flag.astype(jnp.float32) for flag in flags]
 
     def states(part, key_block, count):
+        if isinstance(key_block, tuple):
+            return far_ref[key_block[0], part]
         if count == 1:
             return states_ref[key_block, part]
         return states_ref[pl.ds(key_block, count), part].reshape(count * rows, width)
@@ -285,13 +288,10 @@
                 tiles.append((which, ~n, 1, visible))
         return tiles
 
-    def compute():
-        if step == 1:
-            add([(which, n, 2, None) for which in range(2) for n in range(0, blocks, 2)])
-            return
+    def triangle(own):
         tiles = []
         for n in range(blocks - 1):
-            if step == 0:
+            if own:
                 is_low = n < low
                 tiles.append((jnp.where(is_low, 0, 1), jnp.where(is_low, n, n - low), 1, None))
             else:
@@ -299,9 +299,19 @@
                 tiles.append(
                     (jnp.where(is_high, 1, 0), jnp.where(is_high, high + 1 + n, n + 1), 1, None)
                 )
-
-        for which, block in ((0, low), (1, high)):
-            tiles.append((which, block, 1, in_order))
+        return tiles + [(0, low, 1, in_order), (1, high, 1, in_order)]
+
+    def compute():
+        if step == 1:
+            tiles = [(which, n, 2, None) for which in range(2) for n in range(0, blocks, 2)]
+            if not joined:
+                add(tiles)
+                return
+            far = [(which, (n,), count, seen) for which, n, count, seen in triangle(False)]
+            pl.when(plane == step)(lambda: add(tiles))
+            pl.when(plane > step)(lambda: add(tiles + far))
+            return
+        tiles = triangle(step == 0)
         if not (steerable and last):
             add(tiles)
             return
@@ -341,7 +351,8 @@
 
 
 def attend(
-    step, scalars, bias, queries, states, carried=None, span_states=None, last=False, states_at=0
+    step, scalars, bias, queries, states, carried=None, far_states=None, span_states=None,
+    last=False, states_at=0,
 ):
     blocks, _, rows, width = queries.shape
     pair = 2
@@ -354,6 +365,9 @@
         in_specs.append(pl.BlockSpec(bias.shape, lambda n: (0, 0)))
     operands += [queries, queries, states]
     in_specs += query_specs(queries) + [whole]
+    if far_states is not None:
+        operands.append(far_states)
+        in_specs.append(pl.BlockSpec(far_states.shape, lambda n: (0, 0, 0, 0)))
     if span_states is not None:
         operands.append(span_states)
         in_specs.append(pl.BlockSpec(span_states.shape, lambda n: (0, 0, 0)))
@@ -371,7 +385,13 @@
     else:
         out_shape, out_specs = [held, held], [held_spec(queries)] * 2
     return pl.pallas_call(
-        functools.partial(attend_kernel, step=step, steerable=bias is not None, last=last),
+        functools.partial(
+            attend_kernel,
+            step=step,
+            steerable=bias is not None,
+            last=last,
+            joined=far_states is not None,
+        ),
         grid=(blocks // 2,),
         in_specs=in_specs,
         out_specs=out_specs,
@@ -460,11 +480,11 @@
     far_b = onward(all_b[:, :2])
     held_b = attend(0, scalars, None, all_b, all_b, states_at=1)
     out_a = attend(
-        2, scalars, bias, both_a, far_a, after(held_a, held_b), span_states, last=True
-    )
-    held_b = attend(1, scalars, None, all_b, all_b, after(held_b, out_a))
+        2, scalars, bias, both_a, far_a, after(held_a, held_b), span_states=span_states, last=True
+    )
+    held_b = after(held_b, out_a)
     out_a = exchange(out_a)
-    out_b = attend(2, scalars, None, all_b, far_b, held_b, last=True)
+    out_b = attend(1, scalars, None, all_b, all_b, held_b, far_states=far_b, last=True)
     out_b = exchange(out_b)
     return unpack(scalars, out_a, out_b)
 

time: 164 us -> 164 us (level)
  waiting for transfers between devices: 39.9 us -> 45.2 us
  Pallas kernels: 76.1 us -> 72.8 us
    ppermute x5, waiting for transfers between devices: 11.3 us -> 16.5 us  [onward(): return lax.ppermute(blocks, 'seq', pairs)]
    pallas_call x6 -> x5, Pallas kernels: 66.8 us -> 63.5 us  [attend(): pl.pallas_call(functools.partial(attend_kernel, step=step, steerable=bias...]
  transfers between devices with their start and end apart: 8 -> 8, of which waited for: 4 -> 5; matrix products, arithmetic and copies ran while one was open for 4% -> 4% of each run, Pallas kernels for 41% -> 39%
where the time goes in v3:
time: 164 us
  Pallas kernels  72.8 us (44%)
  waiting for transfers between devices  45.2 us (28%)
  starting transfers between devices  18.8 us (11%)
  blocking collectives  18.4 us (11%)
  local copies, waits for them, and re-layouts  7.47 us (5%)
    pallas_call x5, Pallas kernels, attend(): pl.pallas_call(functools.partial(attend_kernel, step=step, steerable=bias...  63.5 us
    all_to_all x3, waiting for transfers between devices, exchange(): lax.all_to_all(blocks, 'seq', split_axis=0, concat_axis=0, axis_index_gro...  28.7 us
    all_to_all x1, blocking collectives, exchange(): lax.all_to_all(blocks, 'seq', split_axis=0, concat_axis=0, axis_index_gro...  18.4 us
    ppermute x5, waiting for transfers between devices, onward(): return lax.ppermute(blocks, 'seq', pairs)  16.5 us
    all_to_all x3, starting transfers between devices, exchange(): lax.all_to_all(blocks, 'seq', split_axis=0, concat_axis=0, axis_index_gro...  12.2 us
    ppermute x5, starting transfers between devices, onward(): return lax.ppermute(blocks, 'seq', pairs)  6.61 us
    pallas_call x1, Pallas kernels, pack(): pl.pallas_call(pack_kernel, grid=(TOKEN_STEPS,), in_specs=[smem()] * 3 +...  6.5 us
  transfers between devices with their start and end apart: 8, of which 5 were waited for; matrix products, arithmetic and copies ran while one was open for 4% of the time, Pallas kernels for 39%

profile of v3, /device:TPU:24, one launch (start us, length us, event | category | flops | bytes accessed | tf_op | source)
XLA Modules:
  0.0 163.5 jit_solution(12139200419037605047)
XLA Ops:
  0.7 0.0 copy-start
  0.7 0.6 copy-done
  1.3 6.5 %shard_map.55 = (bf16[8,4,256,128]{3,2,1,0:T(8,128)(2,1)}, bf16[8,2,256,128]{3,2,1,0:T(8,128)(2,1)}, bf16[8,6,256,128]{3,2,1,0:T(8,128)(2,1)}, s32[36]{0:T(128)S(1)}) custom-call(s32[1]{0:T(128)} %bitcast.index_ref, s32[1]{0:T(128)} %copy.8.span_ref, s32[8]{0:T(128)S(1)} %copy-done, bf16[256,32,128]{2,1,0:T(8,128)(2,1)} %queries_ref.1, ...), custom_call_target="tpu_custom_call" | custom-call | bytes 8388608 | tf_op jit(solution)/shard_map/pallas_call | solution.py:108
  7.8 0.0 copy-start.2
  7.8 3.9 %all-to-all-start = ((bf16[8,4,256,128]{3,2,1,0:T(8,128)(2,1)}), bf16[8,4,256,128]{3,2,1,0:T(8,128)(2,1)S(1)}, u32[]{:S(2)}, u32[]{:S(2)}) async-start(bf16[8,4,256,128]{3,2,1,0:T(8,128)(2,1)} %get-tuple-element.26), calls=%async_computation | async-start | bytes 4194304 | tf_op jit(solution)/shard_map/all_to_all | solution.py:441
  11.7 0.0 copy-done.2
  11.7 1.3 collective-permute-start
  13.0 25.3 %all-to-all-done.refs_2_.refs_3_.refs_4_ = bf16[8,4,256,128]{3,2,1,0:T(8,128)(2,1)S(1)} async-done(((bf16[8,4,256,128]{3,2,1,0:T(8,128)(2,1)}), bf16[8,4,256,128]{3,2,1,0:T(8,128)(2,1)S(1)}, u32[]{:S(2)}, u32[]{:S(2)}) %all-to-all-start) | async-done | bytes 2097184 | tf_op jit(solution)/shard_map/all_to_all | solution.py:441
  38.3 1.1 slice.12
  39.4 0.0 collective-permute-done
  39.4 1.3 collective-permute-start.1
  40.7 2.5 %constant_dynamic-update-slice_fusion = bf16[8,6,256,128]{3,2,1,0:T(8,128)(2,1)} fusion(bf16[8,6,256,128]{3,2,1,0:T(8,128)(2,1)} %get-tuple-element.36, bf16[8,2,256,128]{3,2,1,0:T(8,128)(2,1)} %collective-permute-done), kind=kLoop, calls=%fused_computation.5 | loop fusion | bytes 2097152 | tf_op jit(solution)/shard_map/dynamic_update_slice | solution.py:467
  43.1 0.0 copy-start.1
  43.1 4.6 %all-to-all-start.1 = ((bf16[8,6,256,128]{3,2,1,0:T(8,128)(2,1)}), bf16[8,6,256,128]{3,2,1,0:T(8,128)(2,1)}, u32[]{:S(2)}, u32[]{:S(2)}) async-start(bf16[8,6,256,128]{3,2,1,0:T(8,128)(2,1)} %constant_dynamic-update-slice_fusion), calls=%async_computation.1 | async-start | bytes 6291456 | tf_op jit(solution)/shard_map/all_to_all | solution.py:441
  47.7 0.0 copy-done.1
  47.8 8.8 %shard_map.56 = (f32[4,2,512,128]{3,2,1,0:T(8,128)}, f32[4,2,512,128]{3,2,1,0:T(8,128)}) custom-call(s32[36]{0:T(128)S(1)} %get-tuple-element.25.refs_0_.scalars, f32[32,256]{1,0:T(8,128)S(1)} %reshape.10.refs_1_, bf16[8,4,256,128]{3,2,1,0:T(8,128)(2,1)S(1)} %all-to-all-done.refs_2_.refs_3_.refs_4_, ...), custom_call_target="tpu_custom_call" | custom-call | flops 1073741824 | bytes 12582912 | tf_op jit(solution)/shard_map/pallas_call | solution.py:387
  56.6 9.5 %collective-permute-done.1.refs_4_ = bf16[8,2,256,128]{3,2,1,0:T(8,128)(2,1)S(1)} collective-permute-done((bf16[8,2,256,128]{3,2,1,0:T(8,128)(2,1)}, bf16[8,2,256,128]{3,2,1,0:T(8,128)(2,1)S(1)}, u32[]{:S(2)}, u32[]{:S(2)}) %collective-permute-start.1) | collective-permute-done | bytes 1048608 | tf_op jit(solution)/shard_map/ppermute | solution.py:448
  66.1 0.1 slice_bitcast_fusion
  66.2 0.1 copy.6
  66.3 0.8 constant_dynamic-slice_fusion
  67.0 1.3 collective-permute-start.3
  68.3 1.3 collective-permute-start.2
  69.6 12.6 %shard_map.57 = (f32[4,2,512,128]{3,2,1,0:T(8,128)}, f32[4,2,512,128]{3,2,1,0:T(8,128)}) custom-call(s32[36]{0:T(128)S(1)} %get-tuple-element.25.refs_0_.scalars, f32[32,256]{1,0:T(8,128)S(1)} %reshape.10.refs_1_, bf16[8,4,256,128]{3,2,1,0:T(8,128)(2,1)S(1)} %all-to-all-done.refs_2_.refs_3_.refs_4_, ...), custom_call_target="tpu_custom_call" | custom-call | flops 17179869184 | bytes 12582912 | tf_op jit(solution)/shard_map/pallas_call | solution.py:387
  82.3 3.4 %all-to-all-done.1.refs_1_.refs_2_.refs_3_ = bf16[8,6,256,128]{3,2,1,0:T(8,128)(2,1)} async-done(((bf16[8,6,256,128]{3,2,1,0:T(8,128)(2,1)}), bf16[8,6,256,128]{3,2,1,0:T(8,128)(2,1)}, u32[]{:S(2)}, u32[]{:S(2)}) %all-to-all-start.1) | async-done | bytes 3145760 | tf_op jit(solution)/shard_map/all_to_all | solution.py:441
  85.6 2.3 %slice.11 = bf16[8,2,256,128]{3,2,1,0:T(8,128)(2,1)} slice(bf16[8,6,256,128]{3,2,1,0:T(8,128)(2,1)} %all-to-all-done.1.refs_1_.refs_2_.refs_3_), slice={[0:8], [0:2], [0:256], [0:128]} | slice | bytes 2097152 | tf_op jit(solution)/shard_map/slice | solution.py:480
  88.0 1.5 collective-permute-start.4
  89.4 9.5 %shard_map.58 = (f32[4,2,512,128]{3,2,1,0:T(8,128)}, f32[4,2,512,128]{3,2,1,0:T(8,128)}) custom-call(s32[36]{0:T(128)S(1)} %get-tuple-element.25.refs_0_.scalars, bf16[8,6,256,128]{3,2,1,0:T(8,128)(2,1)} %all-to-all-done.1.refs_1_.refs_2_.refs_3_, bf16[8,6,256,128]{3,2,1,0:T(8,128)(2,1)} %all-to-all-done.1.refs_1_.refs_2_.refs_3_, ...), custom_call_target="tpu_custom_call" | custom-call | flops 1073741824 | bytes 16777216 | tf_op jit(solution)/shard_map/pallas_call | solution.py:387
  99.0 0.0 collective-permute-done.3.refs_5_
  99.0 1.7 %collective-permute-done.2.refs_4_ = bf16[8,2,256,128]{3,2,1,0:T(8,128)(2,1)} collective-permute-done((bf16[8,2,256,128]{3,2,1,0:T(8,128)(2,1)S(1)}, bf16[8,2,256,128]{3,2,1,0:T(8,128)(2,1)}, u32[]{:S(2)}, u32[]{:S(2)}) %collective-permute-start.2) | collective-permute-done | bytes 1048608 | tf_op jit(solution)/shard_map/ppermute | solution.py:448
  100.6 12.4 %shard_map.59 = bf16[8,2,256,128]{3,2,1,0:T(8,128)(2,1)} custom-call(s32[36]{0:T(128)S(1)} %get-tuple-element.25.refs_0_.scalars, f32[32,256]{1,0:T(8,128)S(1)} %reshape.10.refs_1_, bf16[8,4,256,128]{3,2,1,0:T(8,128)(2,1)S(1)} %all-to-all-done.refs_2_.refs_3_.refs_4_, bf16[8,4,256,128]{3,2,1,0:T(8,128)(2,1)S(1)} %all-to-all-done.refs_2_.refs_3_.refs_4_, ...), custom_call_target="tpu_custom_call" | custom-call | flops 1073741824 | bytes 12582912 | tf_op jit(solution)/shard_map/pallas_call | solution.py:387
  113.1 3.8 %all-to-all-start.2 = ((bf16[8,2,256,128]{3,2,1,0:T(8,128)(2,1)}), bf16[8,2,256,128]{3,2,1,0:T(8,128)(2,1)S(1)}, u32[]{:S(2)}, u32[]{:S(2)}) async-start(bf16[8,2,256,128]{3,2,1,0:T(8,128)(2,1)} %shard_map.59), calls=%async_computation.2 | async-start | bytes 2097152 | tf_op jit(solution)/shard_map/all_to_all | solution.py:441
  116.8 5.3 %collective-permute-done.4.refs_4_ = bf16[8,2,256,128]{3,2,1,0:T(8,128)(2,1)} collective-permute-done((bf16[8,2,256,128]{3,2,1,0:T(8,128)(2,1)}, bf16[8,2,256,128]{3,2,1,0:T(8,128)(2,1)}, u32[]{:S(2)}, u32[]{:S(2)}) %collective-permute-start.4) | collective-permute-done | bytes 1048608 | tf_op jit(solution)/shard_map/ppermute | solution.py:448
  122.2 20.1 %shard_map.60 = bf16[8,2,256,128]{3,2,1,0:T(8,128)(2,1)S(1)} custom-call(s32[36]{0:T(128)S(1)} %get-tuple-element.25.refs_0_.scalars, bf16[8,6,256,128]{3,2,1,0:T(8,128)(2,1)} %all-to-all-done.1.refs_1_.refs_2_.refs_3_, bf16[8,6,256,128]{3,2,1,0:T(8,128)(2,1)} %all-to-all-done.1.refs_1_.refs_2_.refs_3_, ...), custom_call_target="tpu_custom_call" | custom-call | flops 1073741824 | bytes 16777216 | tf_op jit(solution)/shard_map/pallas_call | solution.py:387
  142.3 0.0 all-to-all-done.2.out_a
  142.3 18.4 %all_to_all.20.out_b = bf16[8,2,256,128]{3,2,1,0:T(8,128)(2,1)S(1)} all-to-all(bf16[8,2,256,128]{3,2,1,0:T(8,128)(2,1)S(1)} %shard_map.60), channel_id=1, replica_groups={{0,1,2,3,4,5,6,7},{8,9,10,11,12,13,14,15},{16,17,18,19,20,21,22,23},{24..., dimensions={0} | all-to-all | bytes 2097152 | tf_op jit(solution)/shard_map/all_to_all | solution.py:441
  160.7 2.8 %shard_map.61 = bf16[256,32,128]{2,1,0:T(8,128)(2,1)} custom-call(s32[36]{0:T(128)S(1)} %get-tuple-element.25.refs_0_.scalars, bf16[8,2,256,128]{3,2,1,0:T(8,128)(2,1)S(1)} %all-to-all-done.2.out_a, bf16[8,2,256,128]{3,2,1,0:T(8,128)(2,1)S(1)} %all_to_all.20.out_b), custom_call_target="tpu_custom_call" | custom-call | bytes 4194304 | tf_op jit(solution)/shard_map/pallas_call | solution.py:419
  (2 shorter events, 0.0 us)
Async XLA Ops:
  0.7 0.7 copy-start
  7.8 3.9 %copy-start.2 = (bf16[8,2,256,128]{3,2,1,0:T(8,128)(2,1)S(1)}, bf16[8,2,256,128]{3,2,1,0:T(8,128)(2,1)}, u32[]{:S(2)}) copy-start(bf16[8,2,256,128]{3,2,1,0:T(8,128)(2,1)} %get-tuple-element.27) | copy-start | bytes 3145732
  7.8 30.5 %all-to-all-start = ((bf16[8,4,256,128]{3,2,1,0:T(8,128)(2,1)}), bf16[8,4,256,128]{3,2,1,0:T(8,128)(2,1)S(1)}, u32[]{:S(2)}, u32[]{:S(2)}) async-start(bf16[8,4,256,128]{3,2,1,0:T(8,128)(2,1)} %get-tuple-element.26), calls=%async_computation | async-start | bytes 4194304 | tf_op jit(solution)/shard_map/all_to_all | solution.py:441
  11.7 27.7 %collective-permute-start = (bf16[8,2,256,128]{3,2,1,0:T(8,128)(2,1)S(1)}, bf16[8,2,256,128]{3,2,1,0:T(8,128)(2,1)}, u32[]{:S(2)}, u32[]{:S(2)}) collective-permute-start(bf16[8,2,256,128]{3,2,1,0:T(8,128)(2,1)S(1)} %copy-done.2), channel_id=1, source_target_pairs={{0,8},{1,9},{2,10},{3,11},{4,12},{5,13},{6,14},{7,15},{8,16},{9,17... | collective-permute-start | bytes 3145736 | tf_op jit(solution)/shard_map/ppermute | solution.py:448
  39.4 26.7 %collective-permute-start.1 = (bf16[8,2,256,128]{3,2,1,0:T(8,128)(2,1)}, bf16[8,2,256,128]{3,2,1,0:T(8,128)(2,1)S(1)}, u32[]{:S(2)}, u32[]{:S(2)}) collective-permute-start(bf16[8,2,256,128]{3,2,1,0:T(8,128)(2,1)} %slice.12), channel_id=1, source_target_pairs={{0,8},{1,9},{2,10},{3,11},{4,12},{5,13},{6,14},{7,15},{8,16},{9,17... | collective-permute-start | bytes 3145736 | tf_op jit(solution)/shard_map/ppermute | solution.py:448
  43.1 4.6 %copy-start.1 = (bf16[8192]{0:T(1024)(128)(2,1)S(1)}, bf16[8192]{0:T(1024)(128)(2,1)}, u32[]{:S(2)}) copy-start(bf16[8192]{0:T(1024)(128)(2,1)} %param.7) | copy-start | bytes 49156
  43.1 42.5 %all-to-all-start.1 = ((bf16[8,6,256,128]{3,2,1,0:T(8,128)(2,1)}), bf16[8,6,256,128]{3,2,1,0:T(8,128)(2,1)}, u32[]{:S(2)}, u32[]{:S(2)}) async-start(bf16[8,6,256,128]{3,2,1,0:T(8,128)(2,1)} %constant_dynamic-update-slice_fusion), calls=%async_computation.1 | async-start | bytes 6291456 | tf_op jit(solution)/shard_map/all_to_all | solution.py:441
  67.0 31.9 %collective-permute-start.3 = (bf16[2,512,128]{2,1,0:T(8,128)(2,1)}, bf16[2,512,128]{2,1,0:T(8,128)(2,1)S(1)}, u32[]{:S(2)}, u32[]{:S(2)}) collective-permute-start(bf16[2,512,128]{2,1,0:T(8,128)(2,1)} %constant_dynamic-slice_fusion), channel_id=1, source_target_pairs={{0,24},{1,25},{2,26},{3,27},{4,28},{5,29},{6,30},{7,31}} | collective-permute-start | bytes 786440 | tf_op jit(solution)/shard_map/ppermute | solution.py:448
  68.3 32.3 %collective-permute-start.2 = (bf16[8,2,256,128]{3,2,1,0:T(8,128)(2,1)S(1)}, bf16[8,2,256,128]{3,2,1,0:T(8,128)(2,1)}, u32[]{:S(2)}, u32[]{:S(2)}) collective-permute-start(bf16[8,2,256,128]{3,2,1,0:T(8,128)(2,1)S(1)} %collective-permute-done.1.refs_4_), channel_id=1, source_target_pairs={{0,8},{1,9},{2,10},{3,11},{4,12},{5,13},{6,14},{7,15},{8,16},{9,17... | collective-permute-start | bytes 3145736 | tf_op jit(solution)/shard_map/ppermute | solution.py:448
  88.0 34.2 %collective-permute-start.4 = (bf16[8,2,256,128]{3,2,1,0:T(8,128)(2,1)}, bf16[8,2,256,128]{3,2,1,0:T(8,128)(2,1)}, u32[]{:S(2)}, u32[]{:S(2)}) collective-permute-start(bf16[8,2,256,128]{3,2,1,0:T(8,128)(2,1)} %slice.11), channel_id=1, source_target_pairs={{0,8},{1,9},{2,10},{3,11},{4,12},{5,13},{6,14},{7,15},{8,16},{9,17... | collective-permute-start | bytes 3145736 | tf_op jit(solution)/shard_map/ppermute | solution.py:448
  113.1 29.2 %all-to-all-start.2 = ((bf16[8,2,256,128]{3,2,1,0:T(8,128)(2,1)}), bf16[8,2,256,128]{3,2,1,0:T(8,128)(2,1)S(1)}, u32[]{:S(2)}, u32[]{:S(2)}) async-start(bf16[8,2,256,128]{3,2,1,0:T(8,128)(2,1)} %shard_map.59), calls=%async_computation.2 | async-start | bytes 2097152 | tf_op jit(solution)/shard_map/all_to_all | solution.py:441

commit v4 on v3

--- a/solution.py
+++ b/solution.py
@@ -405,6 +405,51 @@
     )(*operands)
 
 
+def copy_parts(source_of, target_of, sems):
+    copies = [
+        pltpu.make_async_copy(source_of(n), target_of(n), sems.at[n]) for n in range(GROUP)
+    ]
+    for copy in copies:
+        copy.start()
+    for copy in copies:
+        copy.wait()
+
+
+def insert_kernel(parts_ref, whole_ref, result_ref, sems):
+    del whole_ref
+    copy_parts(lambda n: parts_ref.at[n], lambda n: result_ref.at[n, pl.ds(0, 2)], sems)
+
+
+def insert_parts(parts, whole):
+    return pl.pallas_call(
+        insert_kernel,
+        in_specs=[pl.BlockSpec(memory_space=pltpu.HBM)] * 2,
+        out_specs=pl.BlockSpec(memory_space=pltpu.HBM),
+        out_shape=pltpu.HBM(whole.shape, whole.dtype),
+        input_output_aliases={1: 0},
+        scratch_shapes=[pltpu.SemaphoreType.DMA((GROUP,))],
+        compiler_params=params(),
+        cost_estimate=cost(0, 2 * parts.size),
+    )(parts, whole)
+
+
+def take_kernel(whole_ref, parts_ref, sems):
+    copy_parts(lambda n: whole_ref.at[n, pl.ds(0, 2)], lambda n: parts_ref.at[n], sems)
+
+
+def take_parts(whole):
+    blocks, _, rows, width = whole.shape
+    return pl.pallas_call(
+        take_kernel,
+        in_specs=[pl.BlockSpec(memory_space=pltpu.HBM)],
+        out_specs=pl.BlockSpec(memory_space=pltpu.HBM),
+        out_shape=pltpu.HBM((blocks, 2, rows, width), whole.dtype),
+        scratch_shapes=[pltpu.SemaphoreType.DMA((GROUP,))],
+        compiler_params=params(),
+        cost_estimate=cost(0, 2 * blocks * 2 * rows * width),
+    )(whole)
+
+
 def unpack_kernel(scalars, out_a, out_b, attention, heads_ref):
     for n in range(GROUP):
         for group_head in range(2):
@@ -464,7 +509,7 @@
     states_a = both_a[:, :2]
     back_a = onward(after(states_a, raw_b))
     held_a = attend(0, scalars, bias, after(both_a, raw_b), both_a)
-    all_b = lax.dynamic_update_slice(all_b, after(raw_b, states_a), (0, 0, 0, 0))
+    all_b = insert_parts(after(raw_b, states_a), all_b)
     all_b = exchange(all_b)
     far_a = onward(after(back_a, held_a))
     length = GROUP * rows
@@ -477,7 +522,7 @@
     span_states = onward(span_states, 3)
     held_a = attend(1, scalars, bias, both_a, back_a, held_a)
     all_b = after(all_b, held_a)
-    far_b = onward(all_b[:, :2])
+    far_b = onward(take_parts(all_b))
     held_b = attend(0, scalars, None, all_b, all_b, states_at=1)
     out_a = attend(
         2, scalars, bias, both_a, far_a, after(held_a, held_b), span_states=span_states, last=True

time: 164 us -> 166 us (1.012)
  waiting for transfers between devices: 45.2 us -> 47.3 us
    ppermute x5, waiting for transfers between devices: 16.5 us -> 21.3 us  [onward(): return lax.ppermute(blocks, 'seq', pairs)]
    unnamed x6 -> x14, local copies, waits for them, and re-layouts: 0.66 us -> 4.2 us
    all_to_all x3, waiting for transfers between devices: 28.7 us -> 26 us  [exchange(): lax.all_to_all(blocks, 'seq', split_axis=0, concat_axis=0, axis_index_gro...]
    dynamic_update_slice x1 -> x0, local copies, waits for them, and re-layouts: 2.45 us -> none  [per_device(): lax.dynamic_update_slice(all_b, after(raw_b, states_a), (0, 0, 0, 0))]
    slice x1 -> x0, local copies, waits for them, and re-layouts: 2.33 us -> none  [per_device(): far_b = onward(all_b[:, :2])]
    pallas_call x5, Pallas kernels: 63.5 us -> 61.4 us  [attend(): pl.pallas_call(functools.partial(attend_kernel, step=step, steerable=bias...]
    pallas_call x0 -> x2, Pallas kernels: none -> 2.07 us  [the longest x1 1.05 us: take_parts(): pl.pallas_call(take_kernel, in_specs=[pl.BlockSpec(memory_space=pltpu.HBM...]
  transfers between devices with their start and end apart: 8 -> 8, of which waited for: 5 -> 5; matrix products, arithmetic and copies ran while one was open for 4% -> 1% of each run, Pallas kernels for 39% -> 38%
where the time goes in v4:
time: 166 us; the launch traced here: 165 us
  Pallas kernels  73.5 us (44%)
  waiting for transfers between devices  47.3 us (28%)
  blocking collectives  18.8 us (11%)
  starting transfers between devices  18.6 us (11%)
  local copies, waits for them, and re-layouts  6.31 us (4%)
    pallas_call x5, Pallas kernels, attend(): pl.pallas_call(functools.partial(attend_kernel, step=step, steerable=bias...  61.4 us
    all_to_all x3, waiting for transfers between devices, exchange(): lax.all_to_all(blocks, 'seq', split_axis=0, concat_axis=0, axis_index_gro...  26 us
    ppermute x5, waiting for transfers between devices, onward(): return lax.ppermute(blocks, 'seq', pairs)  21.3 us
    all_to_all x1, blocking collectives, exchange(): lax.all_to_all(blocks, 'seq', split_axis=0, concat_axis=0, axis_index_gro...  18.8 us
    all_to_all x3, starting transfers between devices, exchange(): lax.all_to_all(blocks, 'seq', split_axis=0, concat_axis=0, axis_index_gro...  11.9 us
    ppermute x5, starting transfers between devices, onward(): return lax.ppermute(blocks, 'seq', pairs)  6.74 us
    pallas_call x1, Pallas kernels, pack(): pl.pallas_call(pack_kernel, grid=(TOKEN_STEPS,), in_specs=[smem()] * 3 +...  6.52 us
    unnamed x14, local copies, waits for them, and re-layouts  4.2 us
  transfers between devices with their start and end apart: 8, of which 5 were waited for; matrix products, arithmetic and copies ran while one was open for 1% of the time, Pallas kernels for 38%

profile of v4, /device:TPU:24, one launch (start us, length us, event | category | flops | bytes accessed | tf_op | source)
XLA Modules:
  0.0 165.4 jit_solution(17305083219826154399)
XLA Ops:
  0.7 0.0 copy-start.5
  0.7 0.6 copy-done.5
  1.3 6.5 %shard_map.55 = (bf16[8,4,256,128]{3,2,1,0:T(8,128)(2,1)}, bf16[8,2,256,128]{3,2,1,0:T(8,128)(2,1)}, bf16[8,6,256,128]{3,2,1,0:T(8,128)(2,1)}, s32[36]{0:T(128)S(1)}) custom-call(s32[1]{0:T(128)} %bitcast.index_ref, s32[1]{0:T(128)} %copy.9.span_ref, s32[8]{0:T(128)S(1)} %copy-done.5, bf16[256,32,128]{2,1,0:T(8,128)(2,1)} %queries_ref.1, ...), custom_call_target="tpu_custom_call" | custom-call | bytes 8388608 | tf_op jit(solution)/shard_map/pallas_call | solution.py:108
  7.8 3.7 %all-to-all-start = ((bf16[8,4,256,128]{3,2,1,0:T(8,128)(2,1)}), bf16[8,4,256,128]{3,2,1,0:T(8,128)(2,1)S(1)}, u32[]{:S(2)}, u32[]{:S(2)}) async-start(bf16[8,4,256,128]{3,2,1,0:T(8,128)(2,1)} %get-tuple-element.26), calls=%async_computation | async-start | bytes 4194304 | tf_op jit(solution)/shard_map/all_to_all | solution.py:486
  11.6 1.3 collective-permute-start
  12.8 25.4 %all-to-all-done.refs_2_.refs_3_.refs_4_ = bf16[8,4,256,128]{3,2,1,0:T(8,128)(2,1)S(1)} async-done(((bf16[8,4,256,128]{3,2,1,0:T(8,128)(2,1)}), bf16[8,4,256,128]{3,2,1,0:T(8,128)(2,1)S(1)}, u32[]{:S(2)}, u32[]{:S(2)}) %all-to-all-start) | async-done | bytes 2097184 | tf_op jit(solution)/shard_map/all_to_all | solution.py:486
  38.2 0.0 copy-start
  38.2 1.1 slice.8
  39.4 0.0 collective-permute-done.parts_ref
  39.4 1.3 collective-permute-start.1
  40.6 1.0 shard_map.58
  41.7 0.0 copy-done
  41.7 0.0 copy-start.6
  41.7 3.7 %all-to-all-start.1 = ((bf16[8,6,256,128]{3,2,1,0:T(8,128)(2,1)}), bf16[8,6,256,128]{3,2,1,0:T(8,128)(2,1)S(1)}, u32[]{:S(2)}, u32[]{:S(2)}) async-start(bf16[8,6,256,128]{3,2,1,0:T(8,128)(2,1)} %shard_map.58), calls=%async_computation.1 | async-start | bytes 6291456 | tf_op jit(solution)/shard_map/all_to_all | solution.py:486
  45.4 0.0 copy-done.6
  45.5 0.0 copy-start.1
  45.5 1.6 copy-done.1
  47.1 8.8 %shard_map.56 = (f32[4,2,512,128]{3,2,1,0:T(8,128)}, f32[4,2,512,128]{3,2,1,0:T(8,128)}) custom-call(s32[36]{0:T(128)S(1)} %get-tuple-element.25.refs_0_.scalars, f32[32,256]{1,0:T(8,128)S(1)} %reshape.10.refs_1_, bf16[8,4,256,128]{3,2,1,0:T(8,128)(2,1)S(1)} %copy-done.1, bf16[8,4,256,128]{3,2,1,0:T(8,128)(2,1)S(1)} %copy-done.1, ...), custom_call_target="tpu_custom_call" | custom-call | flops 1073741824 | bytes 12582912 | tf_op jit(solution)/shard_map/pallas_call | solution.py:387
  55.9 10.3 %collective-permute-done.1.refs_4_ = bf16[8,2,256,128]{3,2,1,0:T(8,128)(2,1)} collective-permute-done((bf16[8,2,256,128]{3,2,1,0:T(8,128)(2,1)}, bf16[8,2,256,128]{3,2,1,0:T(8,128)(2,1)}, u32[]{:S(2)}, u32[]{:S(2)}) %collective-permute-start.1) | collective-permute-done | bytes 1048608 | tf_op jit(solution)/shard_map/ppermute | solution.py:493
  66.2 0.1 slice_bitcast_fusion
  66.3 0.1 copy.7
  66.4 0.8 constant_dynamic-slice_fusion
  67.2 1.3 collective-permute-start.3
  68.5 1.3 collective-permute-start.2
  69.8 12.9 %shard_map.57 = (f32[4,2,512,128]{3,2,1,0:T(8,128)}, f32[4,2,512,128]{3,2,1,0:T(8,128)}) custom-call(s32[36]{0:T(128)S(1)} %get-tuple-element.25.refs_0_.scalars, f32[32,256]{1,0:T(8,128)S(1)} %reshape.10.refs_1_, bf16[8,4,256,128]{3,2,1,0:T(8,128)(2,1)S(1)} %copy-done.1, bf16[8,4,256,128]{3,2,1,0:T(8,128)(2,1)S(1)} %copy-done.1, ...), custom_call_target="tpu_custom_call" | custom-call | flops 17179869184 | bytes 12582912 | tf_op jit(solution)/shard_map/pallas_call | solution.py:387
  82.6 0.7 all-to-all-done.1.refs_1_.refs_2_.refs_3_.whole_ref
  83.3 1.0 shard_map.61
  84.4 0.0 copy-start.2
  84.4 1.6 collective-permute-start.4
  86.0 8.7 %shard_map.59 = (f32[4,2,512,128]{3,2,1,0:T(8,128)}, f32[4,2,512,128]{3,2,1,0:T(8,128)}) custom-call(s32[36]{0:T(128)S(1)} %get-tuple-element.25.refs_0_.scalars, bf16[8,6,256,128]{3,2,1,0:T(8,128)(2,1)S(1)} %all-to-all-done.1.refs_1_.refs_2_.refs_3_.whole_ref, bf16[8,6,256,128]{3,2,1,0:T(8,128)(2,1)S(1)} %all-to-all-done.1.refs_1_.refs_2_.refs_3_.whole_ref, ...), custom_call_target="tpu_custom_call" | custom-call | flops 1073741824 | bytes 16777216 | tf_op jit(solution)/shard_map/pallas_call | solution.py:387
  94.6 0.0 collective-permute-done.3.refs_5_
  94.6 6.1 %collective-permute-done.2.refs_4_ = bf16[8,2,256,128]{3,2,1,0:T(8,128)(2,1)} collective-permute-done((bf16[8,2,256,128]{3,2,1,0:T(8,128)(2,1)}, bf16[8,2,256,128]{3,2,1,0:T(8,128)(2,1)}, u32[]{:S(2)}, u32[]{:S(2)}) %collective-permute-start.2) | collective-permute-done | bytes 1048608 | tf_op jit(solution)/shard_map/ppermute | solution.py:493
  100.7 0.0 copy-done.2
  100.7 11.4 %shard_map.60 = bf16[8,2,256,128]{3,2,1,0:T(8,128)(2,1)S(1)} custom-call(s32[36]{0:T(128)S(1)} %get-tuple-element.25.refs_0_.scalars, f32[32,256]{1,0:T(8,128)S(1)} %reshape.10.refs_1_, bf16[8,4,256,128]{3,2,1,0:T(8,128)(2,1)S(1)} %copy-done.2, bf16[8,4,256,128]{3,2,1,0:T(8,128)(2,1)S(1)} %copy-done.2, ...), custom_call_target="tpu_custom_call" | custom-call | flops 1073741824 | bytes 12582912 | tf_op jit(solution)/shard_map/pallas_call | solution.py:387
  112.2 0.0 copy-start.3
  112.2 1.0 copy-done.3
  113.2 4.5 %all-to-all-start.2 = ((bf16[8,2,256,128]{3,2,1,0:T(8,128)(2,1)}), bf16[8,2,256,128]{3,2,1,0:T(8,128)(2,1)}, u32[]{:S(2)}, u32[]{:S(2)}) async-start(bf16[8,2,256,128]{3,2,1,0:T(8,128)(2,1)} %copy-done.3), calls=%async_computation.2 | async-start | bytes 2097152 | tf_op jit(solution)/shard_map/all_to_all | solution.py:486
  117.6 4.9 %collective-permute-done.4.refs_4_ = bf16[8,2,256,128]{3,2,1,0:T(8,128)(2,1)} collective-permute-done((bf16[8,2,256,128]{3,2,1,0:T(8,128)(2,1)}, bf16[8,2,256,128]{3,2,1,0:T(8,128)(2,1)}, u32[]{:S(2)}, u32[]{:S(2)}) %collective-permute-start.4) | collective-permute-done | bytes 1048608 | tf_op jit(solution)/shard_map/ppermute | solution.py:493
  122.5 19.6 %shard_map.62 = bf16[8,2,256,128]{3,2,1,0:T(8,128)(2,1)S(1)} custom-call(s32[36]{0:T(128)S(1)} %get-tuple-element.25.refs_0_.scalars, bf16[8,6,256,128]{3,2,1,0:T(8,128)(2,1)S(1)} %all-to-all-done.1.refs_1_.refs_2_.refs_3_.whole_ref, bf16[8,6,256,128]{3,2,1,0:T(8,128)(2,1)S(1)} %all-to-all-done.1.refs_1_.refs_2_.refs_3_.whole_ref, ...), custom_call_target="tpu_custom_call" | custom-call | flops 1073741824 | bytes 16777216 | tf_op jit(solution)/shard_map/pallas_call | solution.py:387
  142.1 0.0 copy-start.4
  142.1 1.0 copy-done.4
  143.1 0.0 all-to-all-done.2.out_a
  143.1 18.8 %all_to_all.20.out_b = bf16[8,2,256,128]{3,2,1,0:T(8,128)(2,1)S(1)} all-to-all(bf16[8,2,256,128]{3,2,1,0:T(8,128)(2,1)} %copy-done.4), channel_id=1, replica_groups={{0,1,2,3,4,5,6,7},{8,9,10,11,12,13,14,15},{16,17,18,19,20,21,22,23},{24..., dimensions={0} | all-to-all | bytes 2097152 | tf_op jit(solution)/shard_map/all_to_all | solution.py:486
  161.9 3.5 %shard_map.63 = bf16[256,32,128]{2,1,0:T(8,128)(2,1)} custom-call(s32[36]{0:T(128)S(1)} %get-tuple-element.25.refs_0_.scalars, bf16[8,2,256,128]{3,2,1,0:T(8,128)(2,1)} %all-to-all-done.2.out_a, bf16[8,2,256,128]{3,2,1,0:T(8,128)(2,1)S(1)} %all_to_all.20.out_b), custom_call_target="tpu_custom_call" | custom-call | bytes 4194304 | tf_op jit(solution)/shard_map/pallas_call | solution.py:464
  (2 shorter events, 0.0 us)
Async XLA Ops:
  0.7 0.7 copy-start.5
  7.8 30.4 %all-to-all-start = ((bf16[8,4,256,128]{3,2,1,0:T(8,128)(2,1)}), bf16[8,4,256,128]{3,2,1,0:T(8,128)(2,1)S(1)}, u32[]{:S(2)}, u32[]{:S(2)}) async-start(bf16[8,4,256,128]{3,2,1,0:T(8,128)(2,1)} %get-tuple-element.26), calls=%async_computation | async-start | bytes 4194304 | tf_op jit(solution)/shard_map/all_to_all | solution.py:486
  11.6 27.8 %collective-permute-start = (bf16[8,2,256,128]{3,2,1,0:T(8,128)(2,1)}, bf16[8,2,256,128]{3,2,1,0:T(8,128)(2,1)S(1)}, u32[]{:S(2)}, u32[]{:S(2)}) collective-permute-start(bf16[8,2,256,128]{3,2,1,0:T(8,128)(2,1)} %get-tuple-element.27), channel_id=1, source_target_pairs={{0,8},{1,9},{2,10},{3,11},{4,12},{5,13},{6,14},{7,15},{8,16},{9,17... | collective-permute-start | bytes 3145736 | tf_op jit(solution)/shard_map/ppermute | solution.py:493
  38.2 3.5 %copy-start = (bf16[8,4,256,128]{3,2,1,0:T(8,128)(2,1)}, bf16[8,4,256,128]{3,2,1,0:T(8,128)(2,1)S(1)}, u32[]{:S(2)}) copy-start(bf16[8,4,256,128]{3,2,1,0:T(8,128)(2,1)S(1)} %all-to-all-done.refs_2_.refs_3_.refs_4_) | copy-start | bytes 6291460
  39.4 26.9 %collective-permute-start.1 = (bf16[8,2,256,128]{3,2,1,0:T(8,128)(2,1)}, bf16[8,2,256,128]{3,2,1,0:T(8,128)(2,1)}, u32[]{:S(2)}, u32[]{:S(2)}) collective-permute-start(bf16[8,2,256,128]{3,2,1,0:T(8,128)(2,1)} %slice.8), channel_id=1, source_target_pairs={{0,8},{1,9},{2,10},{3,11},{4,12},{5,13},{6,14},{7,15},{8,16},{9,17... | collective-permute-start | bytes 3145736 | tf_op jit(solution)/shard_map/ppermute | solution.py:493
  41.7 3.7 %copy-start.6 = (bf16[8192]{0:T(1024)(128)(2,1)S(1)}, bf16[8192]{0:T(1024)(128)(2,1)}, u32[]{:S(2)}) copy-start(bf16[8192]{0:T(1024)(128)(2,1)} %param.7) | copy-start | bytes 49156
  41.7 41.6 %all-to-all-start.1 = ((bf16[8,6,256,128]{3,2,1,0:T(8,128)(2,1)}), bf16[8,6,256,128]{3,2,1,0:T(8,128)(2,1)S(1)}, u32[]{:S(2)}, u32[]{:S(2)}) async-start(bf16[8,6,256,128]{3,2,1,0:T(8,128)(2,1)} %shard_map.58), calls=%async_computation.1 | async-start | bytes 6291456 | tf_op jit(solution)/shard_map/all_to_all | solution.py:486
  45.5 1.6 copy-start.1
  67.2 27.5 %collective-permute-start.3 = (bf16[2,512,128]{2,1,0:T(8,128)(2,1)}, bf16[2,512,128]{2,1,0:T(8,128)(2,1)S(1)}, u32[]{:S(2)}, u32[]{:S(2)}) collective-permute-start(bf16[2,512,128]{2,1,0:T(8,128)(2,1)} %constant_dynamic-slice_fusion), channel_id=1, source_target_pairs={{0,24},{1,25},{2,26},{3,27},{4,28},{5,29},{6,30},{7,31}} | collective-permute-start | bytes 786440 | tf_op jit(solution)/shard_map/ppermute | solution.py:493
  68.5 32.3 %collective-permute-start.2 = (bf16[8,2,256,128]{3,2,1,0:T(8,128)(2,1)}, bf16[8,2,256,128]{3,2,1,0:T(8,128)(2,1)}, u32[]{:S(2)}, u32[]{:S(2)}) collective-permute-start(bf16[8,2,256,128]{3,2,1,0:T(8,128)(2,1)} %collective-permute-done.1.refs_4_), channel_id=1, source_target_pairs={{0,8},{1,9},{2,10},{3,11},{4,12},{5,13},{6,14},{7,15},{8,16},{9,17... | collective-permute-start | bytes 3145736 | tf_op jit(solution)/shard_map/ppermute | solution.py:493
  84.4 16.4 %copy-start.2 = (bf16[8,4,256,128]{3,2,1,0:T(8,128)(2,1)S(1)}, bf16[8,4,256,128]{3,2,1,0:T(8,128)(2,1)}, u32[]{:S(2)}) copy-start(bf16[8,4,256,128]{3,2,1,0:T(8,128)(2,1)} %copy-done) | copy-start | bytes 6291460
  84.4 38.1 %collective-permute-start.4 = (bf16[8,2,256,128]{3,2,1,0:T(8,128)(2,1)}, bf16[8,2,256,128]{3,2,1,0:T(8,128)(2,1)}, u32[]{:S(2)}, u32[]{:S(2)}) collective-permute-start(bf16[8,2,256,128]{3,2,1,0:T(8,128)(2,1)} %shard_map.61), channel_id=1, source_target_pairs={{0,8},{1,9},{2,10},{3,11},{4,12},{5,13},{6,14},{7,15},{8,16},{9,17... | collective-permute-start | bytes 3145736 | tf_op jit(solution)/shard_map/ppermute | solution.py:493
  112.2 1.0 copy-start.3
  113.2 29.9 %all-to-all-start.2 = ((bf16[8,2,256,128]{3,2,1,0:T(8,128)(2,1)}), bf16[8,2,256,128]{3,2,1,0:T(8,128)(2,1)}, u32[]{:S(2)}, u32[]{:S(2)}) async-start(bf16[8,2,256,128]{3,2,1,0:T(8,128)(2,1)} %copy-done.3), calls=%async_computation.2 | async-start | bytes 2097152 | tf_op jit(solution)/shard_map/all_to_all | solution.py:486
  142.1 1.0 copy-start.4
